TPU v7x, 32 devices: a whole 2x2x4 slice. The times are simulated.
32 devices in a mesh: expert: 4 (over x, core), shard: 8 (over z, y).
Axes of the slice: x: 2, y: 2, z: 4, core: 2. Of those that a mesh axis runs over, the one named last changes fastest.
Arguments:
- tokens: bfloat16 [8, 1024, 1024], P('shard', 'expert'), may hold values from -6 to 6
- cotangent: bfloat16 [8, 1024, 1024], P('shard', 'expert'), may hold values from -6 to 6
- routes: int32 [8, 1024, 8], P('shard', 'expert'), may hold values from 0 to 15, all different within a row; in each aligned block of 256 rows (0 to 255, 256 to 511, ..., all dimensions but the last counted through in order) at most 136 rows name the same one
- qkv_w: float32 [1024, 2048], P('shard'), may hold values from -0.1875 to 0.1875
- qkv_m: float32 [1024, 2048], P('shard'), may hold values from -48 to 48
- qkv_v: float32 [1024, 2048], P('shard'), may hold values from 294.912 to 1179.648
- out_w: float32 [1024, 1024], P('shard'), may hold values from -2 to 2
- out_m: float32 [1024, 1024], P('shard'), may hold values from -4 to 4
- out_v: float32 [1024, 1024], P('shard'), may hold values from 2.32 to 9.2
- router_w: float32 [1024, 16], P('shard'), may hold values from -0.09375 to 0.09375
- router_m: float32 [1024, 16], P('shard'), may hold values from -384 to 384
- router_v: float32 [1024, 16], P('shard'), may hold values from 19660.8 to 78643.2
- gains: float32 [2, 1024], P(None, 'shard'), may hold values from 0.5 to 1.5
- gains_m: float32 [2, 1024], P(None, 'shard'), may hold values from -80 to 80
- gains_v: float32 [2, 1024], P(None, 'shard'), may hold values from 737.28 to 2949.12
- expert_in: float32 [16, 2, 512, 1024], P('expert', None, 'shard'), may hold values from -0.1875 to 0.1875
- in_m: float32 [16, 2, 512, 1024], P('expert', None, 'shard'), may hold values from -16 to 16
- in_v: float32 [16, 2, 512, 1024], P('expert', None, 'shard'), may hold values from 38.4 to 153.6
- expert_out: float32 [16, 512, 1024], P('expert', 'shard'), may hold values from -1 to 1
- down_m: float32 [16, 512, 1024], P('expert', 'shard'), may hold values from -3 to 3
- down_v: float32 [16, 512, 1024], P('expert', 'shard'), may hold values from 1.216 to 4.864
Outputs:
- output: bfloat16 [8, 1024, 1024], P('shard', 'expert')
- input_grad: float32 [8, 1024, 1024], P('shard', 'expert')
- qkv_m_new: float32 [1024, 2048], P('shard')
- qkv_v_new: float32 [1024, 2048], P('shard')
- qkv_w_new: float32 [1024, 2048], P('shard')
- out_m_new: float32 [1024, 1024], P('shard')
- out_v_new: float32 [1024, 1024], P('shard')
- out_w_new: float32 [1024, 1024], P('shard')
- router_m_new: float32 [1024, 16], P('shard')
- router_v_new: float32 [1024, 16], P('shard')
- router_w_new: float32 [1024, 16], P('shard')
- gains_m_new: float32 [2, 1024], P(None, 'shard')
- gains_v_new: float32 [2, 1024], P(None, 'shard')
- gains_new: float32 [2, 1024], P(None, 'shard')
- in_m_new: float32 [16, 2, 512, 1024], P('expert', None, 'shard')
- in_v_new: float32 [16, 2, 512, 1024], P('expert', None, 'shard')
- expert_in_new: float32 [16, 2, 512, 1024], P('expert', None, 'shard')
- down_m_new: float32 [16, 512, 1024], P('expert', 'shard')
- down_v_new: float32 [16, 512, 1024], P('expert', 'shard')
- expert_out_new: float32 [16, 512, 1024], P('expert', 'shard')
Inputs may be any that keep to these rules, and one draw needn't show every extreme that they name: `routes`: each token names 8 different experts. Among the tokens of one device no expert is named more than 136 times, a bound that some block reaches.
All inputs are finite; a program needn't handle non-finite values.
Results may differ from a plain program's by a relative error of at most 0.028.
Values may be sent and summed in bfloat16 or wider, within the bound.
No kernel may reach another device: no remote copies, remote signals or barrier semaphores. Data moves between devices by JAX's collectives and lax.ppermute only.
A program may use at most 256 MiB of HBM per device.

v0:
```python
import functools
import math

import jax
import jax.numpy as jnp
from jax import lax
from jax.experimental import pallas as pl
from jax.experimental.pallas import tpu as pltpu
from jax.sharding import PartitionSpec as P

D = 1024
HQ = 16
KVH = 8
HD = 64
FF = 512
STEP = 10

EXPERT = ("x", "core")
DEEP = ("far", "near")
SHARD = ("far", "near", "y")
EXTRA = 16
TILE = 256

beta_one = 0.9
beta_two = 0.95
adam_eps = 1e-08
weight_decay = 0.1
norm_eps = 1e-05
rope_base = 10000.0
masked_score = -1e30
low = jnp.bfloat16
high = jnp.float32

SMALL = pl.BlockSpec(memory_space=pltpu.SMEM)
WHOLE = pl.BlockSpec(memory_space=pltpu.VMEM)
NO_COST = pl.CostEstimate(flops=0, bytes_accessed=0, transcendentals=0)
PARAMS = pltpu.CompilerParams(vmem_limit_bytes=56 * 1024 * 1024)


def rms_scale(values):
    return lax.rsqrt(jnp.mean(values * values, axis=-1, keepdims=True) + norm_eps)


def norm_back(values, scale, gain, grad):
    weighted = gain * grad
    inner = jnp.mean(values * weighted, axis=-1, keepdims=True)
    return scale * weighted - values * (scale * scale * scale) * inner


def dot_plain(first, second):
    return jnp.dot(first, second, preferred_element_type=high)


def dot_rows(first, second):
    return lax.dot_general(first, second, (((1,), (1,)), ((), ())), preferred_element_type=high)


def dot_tokens(first, second):
    return lax.dot_general(first, second, (((0,), (0,)), ((), ())), preferred_element_type=high)


def adam_step(weight, first, second, grad, rate, decay):
    new_first = beta_one * first + (1.0 - beta_one) * grad
    new_second = beta_two * second + (1.0 - beta_two) * grad * grad
    fix_one = 1.0 - beta_one**STEP
    fix_two = 1.0 - beta_two**STEP
    update = new_first / fix_one / (jnp.sqrt(new_second / fix_two) + adam_eps)
    return (new_first, new_second, weight - rate * (update + decay * weight))


def rotary_tables(length):
    half = HD // 2
    freqs = rope_base ** (-jnp.arange(half, dtype=high) / half)
    angles = jnp.arange(length, dtype=high)[:, None] * freqs[None, :]
    cosine = jnp.cos(angles)
    sine = jnp.sin(angles)
    return (
        jnp.concatenate([cosine] * 4, axis=1),
        jnp.concatenate([-sine, sine, -sine, sine], axis=1),
    )


def rotary(values, cosine, sine, turned):
    blocks = []
    for start in range(0, values.shape[1], 128):
        block = values[:, start : start + 128]
        count = min(128, turned - start)
        if count > 0:
            lane = lax.broadcasted_iota(jnp.int32, block.shape, 1)
            partner = jnp.where(
                lane % HD < HD // 2,
                pltpu.roll(block, 128 - HD // 2, axis=1),
                pltpu.roll(block, HD // 2, axis=1),
            )
            moved = block * cosine + partner * sine
            block = moved if count == 128 else jnp.where(lane < count, moved, block)
        blocks.append(block)
    return jnp.concatenate(blocks, axis=1)


def causal_tail(scores, filler):
    tile, keys = scores.shape
    row = lax.broadcasted_iota(jnp.int32, scores.shape, 0)
    column = lax.broadcasted_iota(jnp.int32, scores.shape, 1)
    return jnp.where(column <= row + (keys - tile), scores, filler)


def aligned(index, size):
    return pl.ds(pl.multiple_of(index * size, size), size)


def attend_kernel(count, heads, keys, blocks, shards, *refs):
    x_refs = refs[:count]
    w_ref, cos_ref, sin_ref = refs[count : count + 3]
    norm_ref, weight_ref, extra_ref, query_ref, key_ref, value_ref = refs[count + 3 : count + 9]
    out_ref, total_ref, head_out = refs[count + 9 :]
    rows, width = x_refs[0].shape
    length = count * rows
    part = w_ref.shape[1] - EXTRA
    for shard in range(w_ref.shape[0]):
        place = slice(shard * part, (shard + 1) * part)
        slot = shards[shard]
        weight_ref[place, :] = w_ref[slot, :part, :]
        extra_ref[:EXTRA, place] = w_ref[slot, part:, :part]
        extra_ref[EXTRA:, place] = w_ref[slot, part:, part : 2 * part]
    gain = extra_ref[EXTRA : EXTRA + 1, :].astype(high)
    for slot in range(count):
        place = aligned(blocks[slot], rows)
        values = x_refs[slot][...].astype(high)
        normed = (values * rms_scale(values) * gain).astype(low)
        norm_ref[place, :] = normed
        proj = rotary(
            dot_plain(normed, weight_ref[...]),
            cos_ref[place, :],
            sin_ref[place, :],
            (heads + keys) * HD,
        )
        for head in range(heads):
            query_ref[head, place, :] = (proj[:, head * HD : (head + 1) * HD] * 0.125).astype(low)
        for head in range(keys):
            start = (heads + head) * HD
            key_ref[head, place, :] = proj[:, start : start + HD].astype(low)
            start = (heads + keys + head) * HD
            value_ref[head, place, :] = proj[:, start : start + HD].astype(low)

    def one_head(head, carry):
        group = lax.div(head, heads // keys)
        for tile in range(length // TILE):
            place = slice(tile * TILE, (tile + 1) * TILE)
            seen = (tile + 1) * TILE
            scores = dot_rows(query_ref[head, place, :], key_ref[group, :seen, :])
            scores = causal_tail(scores, masked_score)
            peak = jnp.max(scores, axis=-1, keepdims=True)
            weights = jnp.exp(scores - peak)
            total = jnp.sum(weights, axis=-1, keepdims=True)
            total_ref[head, place, :] = peak + jnp.log(total)
            summed = dot_plain(weights.astype(low), value_ref[group, :seen, :])
            head_out[head, place, :] = summed / total
        return carry

    lax.fori_loop(0, heads, one_head, 0)
    for head in range(heads):
        out_ref[:, head * HD : (head + 1) * HD] = head_out[head].astype(low)


def attend(blocks, shards, x_all, w_all, cosine, sine, heads, keys):
    count = len(x_all)
    rows, width = x_all[0].shape
    length = count * rows
    columns = w_all.shape[2]
    return pl.pallas_call(
        functools.partial(attend_kernel, count, heads, keys),
        out_shape=(
            jax.ShapeDtypeStruct((length, width), low),
            jax.ShapeDtypeStruct((width, columns), low),
            jax.ShapeDtypeStruct((2 * EXTRA, width), low),
            jax.ShapeDtypeStruct((heads, length, HD), low),
            jax.ShapeDtypeStruct((keys, length, HD), low),
            jax.ShapeDtypeStruct((keys, length, HD), low),
            jax.ShapeDtypeStruct((length, heads * HD), low),
            jax.ShapeDtypeStruct((heads, length, 1), high),
        ),
        in_specs=[SMALL, SMALL] + [WHOLE] * (count + 3),
        out_specs=[WHOLE] * 8,
        scratch_shapes=[pltpu.VMEM((heads, length, HD), high)],
        compiler_params=PARAMS,
        cost_estimate=NO_COST,
        name="attend",
    )(blocks, shards, *x_all, w_all, cosine, sine)


def project_kernel(blocks, sides, o_ref, w_ref, *refs):
    weight = refs[-1]
    part = w_ref.shape[1]
    for side in range(w_ref.shape[0]):
        weight[side * part : (side + 1) * part, :] = w_ref[sides[side]]
    for slot, out_ref in enumerate(refs[:-1]):
        place = aligned(blocks[slot], out_ref.shape[0])
        out_ref[...] = dot_plain(o_ref[place, :], weight[...]).astype(low)


def project(blocks, sides, attended, w_all, count):
    length, inner = attended.shape
    width = w_all.shape[2]
    return pl.pallas_call(
        project_kernel,
        out_shape=(jax.ShapeDtypeStruct((length // count, width), low),) * count,
        in_specs=[SMALL, SMALL, WHOLE, WHOLE],
        out_specs=[WHOLE] * count,
        scratch_shapes=[pltpu.VMEM((inner, width), low)],
        compiler_params=PARAMS,
        cost_estimate=NO_COST,
        name="project",
    )(blocks, sides, attended, w_all)


def experts_kernel(
    first,
    h_0,
    h_1,
    h_2,
    h_3,
    pack_0,
    pack_1,
    pack_2,
    pack_3,
    router_ref,
    gate_ref,
    up_ref,
    down_ref,
    act_ref,
    gate_grad_ref,
    up_grad_ref,
    logit_ref,
    router_grad_ref,
    *refs,
):
    down_grad_refs = refs[:-4]
    rows_now, pack_now, down_sum, router_sum = refs[-4:]
    step = pl.program_id(0)
    owned, hidden, width = gate_ref.shape
    experts = router_ref.shape[0]

    @pl.when(step == 0)
    def _():
        down_sum[...] = jnp.zeros_like(down_sum)
        router_sum[...] = jnp.zeros_like(router_sum)

    for index, (h_ref, pack_ref) in enumerate(
        ((h_0, pack_0), (h_1, pack_1), (h_2, pack_2), (h_3, pack_3))
    ):

        @pl.when(step == index)
        def _():
            rows_now[...] = h_ref[...]
            pack_now[...] = pack_ref[...]

    rows = rows_now[...]
    grads = pack_now[:, :width]
    chosen = pack_now[:, width : width + experts].astype(high) > 0.5
    logits = jnp.where(chosen, dot_rows(rows, router_ref[...]), masked_score)
    powers = jnp.exp(logits - jnp.max(logits, axis=-1, keepdims=True))
    powers = jnp.where(chosen, powers, 0.0)
    gates = powers / jnp.sum(powers, axis=-1, keepdims=True)
    lane = lax.broadcasted_iota(jnp.int32, gates.shape, 1)
    gate_grads = jnp.zeros_like(gates)
    for expert in range(owned):
        mine = lane == first[0] + expert
        gate = jnp.sum(jnp.where(mine, gates, 0.0), axis=1, keepdims=True)
        place = slice(expert * hidden, (expert + 1) * hidden)
        gate_part = dot_rows(rows, gate_ref[expert])
        up_part = dot_rows(rows, up_ref[expert])
        plain = dot_rows(grads, down_ref[expert])
        sigmoid = 1.0 / (1.0 + jnp.exp(-gate_part))
        swish = gate_part * sigmoid
        active = swish * up_part
        found = jnp.sum(plain * active, axis=1, keepdims=True) * gate
        weighted = (active * gate).astype(low)
        plain = plain * gate
        act_ref[:, place] = weighted
        gate_grad_ref[:, place] = (
            plain * up_part * (sigmoid + swish * (1.0 - sigmoid))
        ).astype(low)
        up_grad_ref[:, place] = (plain * swish).astype(low)
        down_sum[expert] += dot_tokens(weighted, grads)
        gate_grads = gate_grads + jnp.where(mine, found, 0.0)
    logit_grads = gate_grads - gates * jnp.sum(gate_grads, axis=1, keepdims=True)
    logit_grads = logit_grads.astype(low)
    logit_ref[...] = logit_grads
    router_sum[...] += dot_tokens(logit_grads, rows)

    @pl.when(step == pl.num_programs(0) - 1)
    def _():
        unit = hidden // len(down_grad_refs)
        for index, down_grad_ref in enumerate(down_grad_refs):
            down_grad_ref[...] = down_sum[:, index * unit : (index + 1) * unit, :].astype(low)
        router_grad_ref[...] = router_sum[...]


def fixed(*shape):
    return pl.BlockSpec(shape, lambda i: (0,) * len(shape))


def by_tile(tile, columns):
    return pl.BlockSpec((tile, columns), lambda i: (i, 0))


def run_experts(first, h_all, pack_all, router, gate_w, up_w, down_w, units):
    tile, width = h_all[0].shape
    count = tile * len(h_all)
    owned, hidden, _ = gate_w.shape
    experts = router.shape[0]
    inner = owned * hidden
    unit = (owned, hidden // units, width)
    return pl.pallas_call(
        experts_kernel,
        grid=(len(h_all),),
        out_shape=(
            jax.ShapeDtypeStruct((count, inner), low),
            jax.ShapeDtypeStruct((count, inner), low),
            jax.ShapeDtypeStruct((count, inner), low),
            jax.ShapeDtypeStruct((count, experts), low),
            jax.ShapeDtypeStruct((experts, width), high),
        )
        + (jax.ShapeDtypeStruct(unit, low),) * units,
        in_specs=[SMALL]
        + [fixed(tile, width)] * 4
        + [fixed(tile, pack_all[0].shape[1])] * 4
        + [fixed(experts, width)]
        + [fixed(owned, hidden, width)] * 3,
        out_specs=(
            by_tile(tile, inner),
            by_tile(tile, inner),
            by_tile(tile, inner),
            by_tile(tile, experts),
            fixed(experts, width),
        )
        + (fixed(*unit),) * units,
        scratch_shapes=[
            pltpu.VMEM((tile, width), low),
            pltpu.VMEM((tile, pack_all[0].shape[1]), low),
            pltpu.VMEM((owned, hidden, width), high),
            pltpu.VMEM((experts, width), high),
        ],
        compiler_params=PARAMS,
        cost_estimate=NO_COST,
        name="experts",
    )(first, *h_all, *pack_all, router, gate_w, up_w, down_w)


def back_rows_kernel(
    gate_grad_ref, up_grad_ref, logit_ref, gate_ref, up_ref, router_ref, *out_refs
):
    result = (
        dot_plain(gate_grad_ref[...], gate_ref[...])
        + dot_plain(up_grad_ref[...], up_ref[...])
        + dot_plain(logit_ref[...], router_ref[...])
    ).astype(low)
    for index, out_ref in enumerate(out_refs):

        @pl.when(pl.program_id(0) == index)
        def _():
            out_ref[...] = result


def back_rows(gate_grad, up_grad, logit_grad, gate_w, up_w, router):
    count, inner = gate_grad.shape
    width = gate_w.shape[1]
    experts = router.shape[0]
    tile = count // 4
    return pl.pallas_call(
        back_rows_kernel,
        grid=(4,),
        out_shape=(jax.ShapeDtypeStruct((tile, width), low),) * 4,
        in_specs=[
            by_tile(tile, inner),
            by_tile(tile, inner),
            by_tile(tile, experts),
            fixed(inner, width),
            fixed(inner, width),
            fixed(experts, width),
        ],
        out_specs=(fixed(tile, width),) * 4,
        compiler_params=PARAMS,
        cost_estimate=NO_COST,
        name="back_rows",
    )(gate_grad, up_grad, logit_grad, gate_w, up_w, router)


def weight_grads_kernel(grad_ref, h_0, h_1, h_2, h_3, *out_refs):
    tile = h_0.shape[0]
    total = dot_tokens(grad_ref[:tile, :], h_0[...])
    for index, h_ref in enumerate((h_1, h_2, h_3)):
        total = total + dot_tokens(
            grad_ref[(index + 1) * tile : (index + 2) * tile, :], h_ref[...]
        )
    unit = out_refs[0].shape[1]
    for index, out_ref in enumerate(out_refs):
        out_ref[0] = total[index * unit : (index + 1) * unit, :].astype(low)


def weight_grads(grad, h_all, owned, units):
    count, inner = grad.shape
    tile, width = h_all[0].shape
    hidden = inner // owned
    unit = hidden // units
    return pl.pallas_call(
        weight_grads_kernel,
        grid=(owned,),
        out_shape=(jax.ShapeDtypeStruct((owned, unit, width), low),) * units,
        in_specs=[pl.BlockSpec((count, hidden), lambda i: (0, i))] + [fixed(tile, width)] * 4,
        out_specs=(pl.BlockSpec((1, unit, width), lambda i: (i, 0, 0)),) * units,
        compiler_params=PARAMS,
        cost_estimate=NO_COST,
        name="weight_grads",
    )(grad, *h_all)


def results_kernel(act_ref, down_ref, *out_refs):
    result = dot_plain(act_ref[...], down_ref[...]).astype(low)
    for index, out_ref in enumerate(out_refs):

        @pl.when(pl.program_id(0) == index)
        def _():
            out_ref[...] = result


def expert_results(act, down_w):
    count, inner = act.shape
    width = down_w.shape[1]
    tile = count // 4
    return pl.pallas_call(
        results_kernel,
        grid=(4,),
        out_shape=(jax.ShapeDtypeStruct((tile, width), low),) * 4,
        in_specs=[by_tile(tile, inner), fixed(inner, width)],
        out_specs=(fixed(tile, width),) * 4,
        compiler_params=PARAMS,
        cost_estimate=NO_COST,
        name="expert_results",
    )(act, down_w)


def out_grads_kernel(count, wide, blocks, side_at, *refs):
    grad_refs = refs[:count]
    o_ref = refs[count]
    out_refs = refs[count + 1 : count + 1 + wide]
    out_sum = refs[-1]
    rows = grad_refs[0].shape[0]
    part = out_refs[0].shape[0]
    for slot in range(count):
        place = aligned(blocks[slot], rows)
        piece = dot_tokens(o_ref[place, :], grad_refs[slot][...])
        out_sum[...] = piece if slot == 0 else out_sum[...] + piece
    for side in range(wide):
        out_refs[side][...] = out_sum[aligned(side_at[side], part), :].astype(low)


def out_grads(blocks, side_at, grad_all, attended):
    count = len(grad_all)
    width = grad_all[0].shape[1]
    inner = attended.shape[1]
    wide = side_at.shape[0]
    return pl.pallas_call(
        functools.partial(out_grads_kernel, count, wide),
        out_shape=(jax.ShapeDtypeStruct((inner // wide, width), low),) * wide,
        in_specs=[SMALL] * 2 + [WHOLE] * (count + 1),
        out_specs=[WHOLE] * wide,
        scratch_shapes=[pltpu.VMEM((inner, width), high)],
        compiler_params=PARAMS,
        cost_estimate=NO_COST,
        name="out_grads",
    )(blocks, side_at, *grad_all, attended)


def attend_back_kernel(count, heads, keys, sizes, blocks, shard_at, sides, *refs):
    deep, wide = sizes
    grad_refs = refs[:count]
    x_refs = refs[count : 2 * count]
    refs = refs[2 * count :]
    (
        w_ref,
        weight_ref,
        norm_ref,
        query_ref,
        key_ref,
        value_ref,
        o_ref,
        total_ref,
        cos_ref,
        sin_ref,
        router_ref,
        gain_ref,
    ) = refs[:12]
    refs = refs[12:]
    qkv_refs = refs[:wide]
    row_refs = refs[wide : wide + count]
    (
        out_w,
        head_grad,
        head_o,
        query_sum,
        key_sum,
        value_sum,
        proj,
        proj_low,
        gains,
        qkv_sum,
    ) = refs[wide + count :]
    rows, width = x_refs[0].shape
    length = count * rows
    part = w_ref.shape[1]
    for side in range(wide):
        out_w[side * part : (side + 1) * part, :] = w_ref[sides[side]]
    for slot in range(count):
        place = aligned(blocks[slot], rows)
        grad = grad_refs[slot][...]
        spread = dot_rows(grad, out_w[...]).astype(low)
        attended = o_ref[place, :]
        for head in range(heads):
            head_grad[head, place, :] = spread[:, head * HD : (head + 1) * HD]
            head_o[head, place, :] = attended[:, head * HD : (head + 1) * HD]
    key_sum[...] = jnp.zeros_like(key_sum)
    value_sum[...] = jnp.zeros_like(value_sum)

    def one_head(head, carry):
        group = lax.div(head, heads // keys)
        for tile in range(length // TILE):
            place = slice(tile * TILE, (tile + 1) * TILE)
            seen = (tile + 1) * TILE
            query = query_ref[head, place, :]
            key = key_ref[group, :seen, :]
            grad = head_grad[head, place, :]
            scores = dot_rows(query, key) - total_ref[head, place, :]
            probs = jnp.exp(causal_tail(scores, masked_score))
            offset = jnp.sum(
                grad.astype(high) * head_o[head, place, :].astype(high), axis=-1, keepdims=True
            )
            inner = dot_rows(grad, value_ref[group, :seen, :])
            score_grad = (probs * (inner - offset)).astype(low)
            query_sum[head, place, :] = dot_plain(score_grad, key) * 0.125
            key_sum[group, :seen, :] += dot_tokens(score_grad, query)
            value_sum[group, :seen, :] += dot_tokens(probs.astype(low), grad)
        return carry

    lax.fori_loop(0, heads, one_head, 0)
    for head in range(heads):
        proj[:, head * HD : (head + 1) * HD] = query_sum[head]
    for head in range(keys):
        start = (heads + head) * HD
        proj[:, start : start + HD] = key_sum[head]
        start = (heads + keys + head) * HD
        proj[:, start : start + HD] = value_sum[head]
    gains[...] = jnp.zeros_like(gains)
    gains[1:2, :] = gain_ref[...]
    for slot in range(count):
        place = aligned(blocks[slot], rows)
        turned = rotary(
            proj[place, :], cos_ref[place, :], -sin_ref[place, :], (heads + keys) * HD
        ).astype(low)
        proj_low[place, :] = turned
        back = dot_rows(turned, weight_ref[...])
        row_refs[slot][...] = back.astype(low)
        values = x_refs[slot][...].astype(high)
        gains[0:1, :] += jnp.sum(back * (values * rms_scale(values)), axis=0, keepdims=True)
    for start in range(0, width, TILE):
        piece = dot_tokens(norm_ref[:, start : start + TILE], proj_low[...]).astype(low)
        for shard in range(start // part, (start + TILE) // part):
            offset = shard * part - start
            qkv_sum[shard, :part, :] = piece[offset : offset + part, :]
    for shard in range(deep * wide):
        place = slice(shard * part, (shard + 1) * part)
        qkv_sum[shard, part:, :] = jnp.zeros((EXTRA, qkv_sum.shape[2]), low)
        qkv_sum[shard, part:, :part] = router_ref[:, place].astype(low)
        qkv_sum[shard, part:, part : 2 * part] = gains[:, place].astype(low)
    for side in range(wide):
        for step in range(deep):
            qkv_refs[side][step] = qkv_sum[shard_at[side * deep + step]]


def attend_back(
    blocks,
    shard_at,
    sides,
    grad_all,
    x_all,
    w_all,
    weight,
    normed,
    query,
    key,
    value,
    attended,
    totals,
    cosine,
    sine,
    router_grad,
    gain_grad,
):
    count = len(x_all)
    rows, width = x_all[0].shape
    length = count * rows
    heads = query.shape[0]
    keys = key.shape[0]
    columns = weight.shape[1]
    wide, part, _ = w_all.shape
    deep = width // (part * wide)
    found = pl.pallas_call(
        functools.partial(attend_back_kernel, count, heads, keys, (deep, wide)),
        out_shape=(jax.ShapeDtypeStruct((deep, part + EXTRA, columns), low),) * wide
        + (jax.ShapeDtypeStruct((rows, width), low),) * count,
        in_specs=[SMALL] * 3 + [WHOLE] * (2 * count + 12),
        out_specs=[WHOLE] * (wide + count),
        scratch_shapes=[
            pltpu.VMEM((heads * HD, width), low),
            pltpu.VMEM((heads, length, HD), low),
            pltpu.VMEM((heads, length, HD), low),
            pltpu.VMEM((heads, length, HD), high),
            pltpu.VMEM((keys, length, HD), high),
            pltpu.VMEM((keys, length, HD), high),
            pltpu.VMEM((length, columns), high),
            pltpu.VMEM((length, columns), low),
            pltpu.VMEM((EXTRA, width), high),
            pltpu.VMEM((deep * wide, part + EXTRA, columns), low),
        ],
        compiler_params=PARAMS,
        cost_estimate=NO_COST,
        name="attend_back",
    )(
        blocks,
        shard_at,
        sides,
        *grad_all,
        *x_all,
        w_all,
        weight,
        normed,
        query,
        key,
        value,
        attended,
        totals,
        cosine,
        sine,
        router_grad,
        gain_grad,
    )
    return found[:wide], found[wide:]


def qkv_step_kernel(rate, slots, g_ref, w_ref, m_ref, v_ref, m_out, v_out, w_out, extra_ref):
    count, whole, columns = g_ref.shape
    part = whole - EXTRA
    rows = aligned(pl.program_id(0), w_ref.shape[0])
    query = HQ * HD // count
    other = KVH * HD // count
    spans = (
        (0, query, 0),
        (query, other, HQ * HD),
        (query + other, other, HQ * HD + KVH * HD),
    )
    total = jnp.zeros((EXTRA, columns), high)
    for block in range(count):
        slot = slots[block]
        total = total + g_ref[slot, part:, :].astype(high)
        for start, size, base in spans:
            place = slice(base + block * size, base + (block + 1) * size)
            first, second, weight = adam_step(
                w_ref[:, place],
                m_ref[:, place],
                v_ref[:, place],
                g_ref[slot, rows, start : start + size].astype(high),
                rate,
                weight_decay,
            )
            m_out[:, place] = first
            v_out[:, place] = second
            w_out[:, place] = weight
    extra_ref[...] = total


def qkv_step(rate, slots, grads, weight, first, second):
    like = jax.ShapeDtypeStruct(weight.shape, high)
    part, columns = weight.shape
    block = by_tile(32, columns)
    return pl.pallas_call(
        functools.partial(qkv_step_kernel, rate),
        grid=(part // 32,),
        out_shape=(like, like, like, jax.ShapeDtypeStruct((EXTRA, grads.shape[2]), high)),
        in_specs=[SMALL, fixed(*grads.shape), block, block, block],
        out_specs=(block, block, block, fixed(EXTRA, grads.shape[2])),
        compiler_params=PARAMS,
        cost_estimate=NO_COST,
        name="qkv_step",
    )(slots, grads, weight, first, second)


def shifted(value, axis, step):
    size = lax.axis_size(axis)
    return lax.ppermute(value, axis, [(j, (j + step) % size) for j in range(size)])


def after(value, *others):
    return lax.optimization_barrier((value, *others))[0]


def collect(value, axis):
    return [value] + [shifted(value, axis, step) for step in range(1, lax.axis_size(axis))]


def give_back(pieces, axis, others=()):
    total = pieces[0].astype(high)
    for step in range(1, lax.axis_size(axis)):
        total = total + after(shifted(pieces[step], axis, -step), *others).astype(high)
    return total.astype(low)


def collect_rows(rows, axis):
    return jnp.concatenate(collect(rows, axis), axis=0)


def collect_first(value):
    half = value.shape[0] // 2
    return collect_rows(value[:half], "x"), collect_rows(value[half:], "near")


def collect_second(upper, lower):
    return collect_rows(upper, "near"), collect_rows(lower, "x")


def collect_core(upper, lower):
    return [upper, lower, shifted(upper, "core", 1), shifted(lower, "core", 1)]


def give_back_chip(pieces):
    return (
        give_back([pieces[0], pieces[2]], "core"),
        give_back([pieces[1], pieces[3]], "core"),
    )


def give_back_rows(rows, axis, others=()):
    return give_back(rows.reshape(lax.axis_size(axis), -1, rows.shape[-1]), axis, others)


def give_back_first(upper, lower):
    return give_back_rows(upper, "near"), give_back_rows(lower, "x")


def give_back_second(upper, lower):
    return jnp.concatenate(
        [give_back_rows(upper, "x"), give_back_rows(lower, "near")], axis=0
    )


def collect_expert(value):
    pieces = collect(value, "x")
    return pieces + [shifted(piece, "core", 1) for piece in pieces]


def give_back_core(pieces):
    half = len(pieces) // 2
    return [give_back([pieces[step], pieces[half + step]], "core") for step in range(half)]


def collect_deep(shard):
    return lax.all_gather(shard.astype(low), "far", axis=1, tiled=True)


def collect_weight(shard):
    return jnp.concatenate(collect(shard, "y"), axis=1)


def give_back_weight(units, *others):
    total = give_back(units, "y", others)
    return lax.psum_scatter(total, "far", scatter_dimension=1, tiled=True)


def diagonal_moves(to_expert):
    size = lax.axis_size(DEEP)
    for step in range(1, size):
        yield [
            (i * size + i, j * size + i if to_expert else i * size + j)
            for i in range(size)
            for j in [(i + step) % size]
        ]


def body(
    tokens,
    cotangent,
    routes,
    qkv_w,
    qkv_m,
    qkv_v,
    out_w,
    out_m,
    out_v,
    router_w,
    router_m,
    router_v,
    gains,
    gains_m,
    gains_v,
    expert_in,
    in_m,
    in_v,
    expert_out,
    down_m,
    down_v,
):
    rows = tokens.shape[1]
    width = tokens.shape[2]
    spread = lax.axis_size(EXPERT)
    length = rows * spread
    experts = router_w.shape[1]
    owned = expert_in.shape[0]
    part = qkv_w.shape[0]
    own = lax.axis_index(EXPERT)
    deep = lax.axis_size(DEEP)
    sides = lax.axis_size("y")
    heads = HQ // spread
    keys = KVH // spread
    joint = EXPERT + DEEP
    across = lax.axis_size("x")
    at_x, at_core, at_y = (lax.axis_index(name) for name in ("x", "core", "y"))
    at_z = lax.axis_index(DEEP)

    order = jnp.arange(spread, dtype=jnp.int32)
    slots = (at_core - order % 2) % 2 * across + (at_x - order // 2) % across
    blocks = (at_x - order % across) % across * 2 + (at_core - order // across) % 2
    order = jnp.arange(deep * sides, dtype=jnp.int32)
    shards = (at_y - order % sides) % sides * deep + (at_z - order // sides) % deep
    shard_at = (at_z - order % deep) % deep * sides + (at_y - order // deep) % sides
    order = jnp.arange(sides, dtype=jnp.int32)
    side_slots = (at_y - order) % sides

    def own_columns(start, size):
        return lax.dynamic_slice_in_dim(qkv_w, start + own * size, size, axis=1).astype(low)

    own_w = jnp.concatenate(
        [
            own_columns(0, heads * HD),
            own_columns(HQ * HD, keys * HD),
            own_columns((HQ + KVH) * HD, keys * HD),
        ],
        axis=1,
    )
    columns = own_w.shape[1]
    own_extra = jnp.concatenate(
        [
            router_w.T.astype(low),
            jnp.pad(gains.astype(low), ((0, EXTRA - 2), (0, columns - 2 * part))),
        ],
        axis=1,
    )
    own_w = jnp.concatenate([own_w, own_extra], axis=0)
    w_deep = jnp.stack(collect(own_w, DEEP))
    w_all = jnp.concatenate(collect(w_deep, "y"), axis=0)
    x_all = collect_expert(tokens[0])
    cosine, sine = rotary_tables(length)

    out_pair = jnp.concatenate(collect(after(out_w.astype(low), w_deep), "y"), axis=0)
    out_pair = after(out_pair, w_all)
    out_all = jnp.where(at_z == own, out_pair, jnp.zeros_like(out_pair))
    for moves in diagonal_moves(False):
        out_all = out_all + lax.ppermute(out_pair, joint, moves)
    out_all = out_all.reshape(sides, part, width)
    gate_deep = collect_deep(expert_in[:, 0])
    up_deep = collect_deep(expert_in[:, 1])
    down_deep = collect_deep(expert_out)
    gate_w = collect_weight(gate_deep)
    hidden = gate_w.shape[1]
    inner = owned * hidden
    chosen = jnp.any(
        routes[0][:, :, None] == jnp.arange(128, dtype=jnp.int32)[None, None, :], axis=1
    )
    pack = collect_first(
        after(jnp.concatenate([cotangent[0], chosen.astype(low)], axis=1), w_all)
    )

    x_all[0] = after(x_all[0], gate_deep)
    normed, weight, extra, query, key, value, attended, totals = attend(
        blocks, shards, x_all, w_all, cosine, sine, heads, keys
    )
    router = extra[:experts]
    gains_all = extra[EXTRA : EXTRA + 2].astype(high)
    gain_one = gains_all[0]
    gain_two = gains_all[1]
    attended, up_deep = lax.optimization_barrier((attended, up_deep))
    pack = collect_second(*lax.optimization_barrier((*pack, attended))[:2])
    branch = give_back(
        give_back_core(project(blocks, side_slots, attended, out_all, spread)), "x"
    )
    inputs = tokens[0].astype(high)
    middle = inputs + after(branch, gate_w, *pack).astype(high)
    scale_two = rms_scale(middle)
    norm_two = (middle * scale_two * gain_two).astype(low)
    up_w = collect_weight(up_deep)
    h_first = lax.optimization_barrier((*collect_first(norm_two), down_deep))
    down_w = collect_weight(h_first[2])
    h_all = collect_core(*collect_second(*h_first[:2]))
    pack_all = collect_core(*pack)

    first = (own * owned).astype(jnp.int32).reshape(1)
    act, gate_grad, up_grad, logit_grad, router_grad, *down_units = run_experts(
        first, h_all, pack_all, router, gate_w, up_w, down_w, sides
    )
    flat_gate = gate_w.reshape(inner, width)
    flat_up = up_w.reshape(inner, width)
    rows_grad = back_rows(gate_grad, up_grad, logit_grad, flat_gate, flat_up, router)
    down_total = give_back_weight(down_units, *rows_grad)
    gate_units = weight_grads(after(gate_grad, *rows_grad), h_all, owned, sides)
    chip_grads = give_back_chip(rows_grad)
    up_units = weight_grads(after(up_grad, gate_units[0], *chip_grads), h_all, owned, sides)
    first_grads = give_back_first(*chip_grads)
    gate_total = give_back_weight(gate_units, *first_grads)
    norm_two_low = give_back_second(*first_grads)
    up_total = give_back_weight(up_units, norm_two_low)
    norm_two_grad = norm_two_low.astype(high)
    results = expert_results(after(act, norm_two_low), down_w.reshape(inner, width))

    out_grad = cotangent[0].astype(high)
    gain_two_grad = jnp.sum(norm_two_grad * middle * scale_two, axis=0, keepdims=True)
    middle_grad = out_grad + norm_back(middle, scale_two, gain_two, norm_two_grad)
    grad_low = middle_grad.astype(low)
    grad_all = collect_expert(grad_low)
    results = lax.optimization_barrier((*results, grad_all[1]))[:4]
    mixed = give_back_chip(results)
    out_units = out_grads(blocks, side_slots, grad_all, attended)
    grad_all[0] = after(grad_all[0], out_units[0], *mixed)
    qkv_grad, norm_one_grad = attend_back(
        blocks,
        shard_at,
        side_slots,
        grad_all,
        x_all,
        out_all,
        weight,
        normed,
        query,
        key,
        value,
        attended,
        totals,
        cosine,
        sine,
        router_grad,
        gain_two_grad,
    )
    qkv_sum = give_back(qkv_grad, "y")
    out_piece = give_back(out_units, "y", qkv_grad)
    norm_one_core = give_back_core(norm_one_grad)
    qkv_total = give_back(after(qkv_sum, *norm_one_core), DEEP)
    upper = give_back_rows(mixed[0], "near", (qkv_total,))
    lower = give_back_rows(mixed[1], "x", (qkv_total,))
    norm_one_low = give_back(norm_one_core, "x", (qkv_total,))
    scale_one = rms_scale(inputs)
    out_total = out_piece.astype(high)
    for moves in diagonal_moves(False):
        moved = lax.ppermute(out_piece, joint, [(b, a) for a, b in moves])
        out_total = out_total + after(moved, qkv_total).astype(high)
    out_piece = out_total.astype(low)
    norm_one_grad = norm_one_low.astype(high)
    input_grad = middle_grad + norm_back(inputs, scale_one, gain_one, norm_one_grad)
    mixed = give_back_second(upper, lower)
    output = (middle + mixed.astype(high)).astype(low)
    qkv_pieces = collect_expert(qkv_total)
    qkv_total = jnp.stack(qkv_pieces)
    out_total = jnp.where(at_z == own, out_piece, jnp.zeros_like(out_piece))
    for moves in diagonal_moves(True):
        out_total = out_total + lax.ppermute(out_piece, joint, moves)
    gate_total = after(gate_total, qkv_pieces[1])

    rate = 3.0 * D ** (-0.5)
    qkv_new_m, qkv_new_v, qkv_new_w, extra_total = qkv_step(
        rate, slots, qkv_total, qkv_w, qkv_m, qkv_v
    )
    router_total = extra_total[:experts, :part].T
    gains_total = extra_total[:2, part : 2 * part]
    in_total = jnp.stack([gate_total, up_total], axis=1)
    rates = (
        3.0 * (HQ * HD * 8 // length) ** (-0.5),
        3.0 * (4 * D) ** (-0.5),
        0.6,
        rate,
        3.0 * (FF // 16) ** (-0.5),
    )
    decays = (weight_decay, weight_decay, 0.0, weight_decay, weight_decay)
    masters = (out_w, router_w, gains, expert_in, expert_out)
    firsts = (out_m, router_m, gains_m, in_m, down_m)
    seconds = (out_v, router_v, gains_v, in_v, down_v)
    grads = (out_total, router_total, gains_total, in_total, down_total)
    updated = [qkv_new_m, qkv_new_v, qkv_new_w]
    for index in range(5):
        updated.extend(
            adam_step(
                masters[index],
                firsts[index],
                seconds[index],
                grads[index].astype(high),
                rates[index],
                decays[index],
            )
        )
    return (output[None], input_grad[None], *updated)


def solution(mesh):
    spread = mesh.shape["expert"]
    shards = mesh.shape["shard"]
    short = math.isqrt(shards // 2)
    grid = jax.sharding.Mesh(
        mesh.devices.reshape(spread // 2, 2, shards // short // 2, 2, short),
        ("x", "core", "far", "near", "y"),
    )
    in_specs = (
        P(SHARD, EXPERT, None),
        P(SHARD, EXPERT, None),
        P(SHARD, EXPERT, None),
        P(SHARD, None),
        P(SHARD, None),
        P(SHARD, None),
        P(SHARD, None),
        P(SHARD, None),
        P(SHARD, None),
        P(SHARD, None),
        P(SHARD, None),
        P(SHARD, None),
        P(None, SHARD),
        P(None, SHARD),
        P(None, SHARD),
        P(EXPERT, None, SHARD, None),
        P(EXPERT, None, SHARD, None),
        P(EXPERT, None, SHARD, None),
        P(EXPERT, SHARD, None),
        P(EXPERT, SHARD, None),
        P(EXPERT, SHARD, None),
    )
    out_specs = (
        P(SHARD, EXPERT, None),
        P(SHARD, EXPERT, None),
        P(SHARD, None),
        P(SHARD, None),
        P(SHARD, None),
        P(SHARD, None),
        P(SHARD, None),
        P(SHARD, None),
        P(SHARD, None),
        P(SHARD, None),
        P(SHARD, None),
        P(None, SHARD),
        P(None, SHARD),
        P(None, SHARD),
        P(EXPERT, None, SHARD, None),
        P(EXPERT, None, SHARD, None),
        P(EXPERT, None, SHARD, None),
        P(EXPERT, SHARD, None),
        P(EXPERT, SHARD, None),
        P(EXPERT, SHARD, None),
    )
    return jax.shard_map(body, mesh=grid, in_specs=in_specs, out_specs=out_specs, check_vma=False)
```

profile of v0, /device:TPU:8, one launch (start us, length us, event | category | flops | bytes accessed | tf_op | source)
XLA Modules:
  0.0 460.9 jit_solution(2994511265698499267)
XLA Ops:
  7.3 2.8 fusion.66
  22.1 2.7 fusion.29
  26.7 16.4 %collective-permute-done.4 = bf16[144,512]{1,0:T(8,128)(2,1)} collective-permute-done((bf16[144,512]{1,0:T(8,128)(2,1)}, bf16[144,512]{1,0:T(8,128)(2,1)}, u32[]{:S(2)}, u32[]{:S(2)}) %collective-permute-start.4) | collective-permute-done | bytes 147488 | tf_op jit(solution)/shard_map/ppermute | solution.py:700
  43.1 5.8 %collective-permute-done.3 = bf16[144,512]{1,0:T(8,128)(2,1)} collective-permute-done((bf16[144,512]{1,0:T(8,128)(2,1)}, bf16[144,512]{1,0:T(8,128)(2,1)}, u32[]{:S(2)}, u32[]{:S(2)}) %collective-permute-start.3) | collective-permute-done | bytes 147488 | tf_op jit(solution)/shard_map/ppermute | solution.py:700
  56.0 10.4 %collective-permute-done.6 = bf16[4,144,512]{2,1,0:T(8,128)(2,1)S(1)} collective-permute-done((bf16[4,144,512]{2,1,0:T(8,128)(2,1)S(1)}, bf16[4,144,512]{2,1,0:T(8,128)(2,1)S(1)}, u32[]{:S(2)}, u32[]{:S(2)}) %collective-permute-start.6) | collective-permute-done | bytes 589856 | tf_op jit(solution)/shard_map/ppermute | solution.py:700
  72.6 9.0 %collective-permute-done.16 = bf16[128,1152]{1,0:T(8,128)(2,1)} collective-permute-done((bf16[128,1152]{1,0:T(8,128)(2,1)S(1)}, bf16[128,1152]{1,0:T(8,128)(2,1)}, u32[]{:S(2)}, u32[]{:S(2)}) %collective-permute-start.16) | collective-permute-done | bytes 294944 | tf_op jit(solution)/shard_map/ppermute | solution.py:700
  88.2 13.7 %attend.1 = (bf16[1024,1024]{1,0:T(8,128)(2,1)}, bf16[1024,512]{1,0:T(8,128)(2,1)}, bf16[32,1024]{1,0:T(8,128)(2,1)}, bf16[4,1024,64]{2,1,0:T(8,128)(2,1)}, bf16...) custom-call(s32[4]{0:T(128)} %fusion.35.blocks, ...), custom_call_target="tpu_custom_call" | custom-call | tf_op jit(solution)/shard_map/attend/pallas_call | solution.py:171
  101.9 6.1 %collective-permute-start.17 = (bf16[256,1152]{1,0:T(8,128)(2,1)S(1)}, bf16[256,1152]{1,0:T(8,128)(2,1)S(1)}, u32[]{:S(2)}, u32[]{:S(2)}) collective-permute-start(bf16[256,1152]{1,0:T(8,128)(2,1)S(1)} %pad_maximum_fusion.4), channel_id=1, source_target_pairs={{0,2},{2,0},{1,3},{3,1},{4,6},{6,4},{5,7},{7,5},{8,10},{10,8},{9,1... | collective-permute-start | bytes 1769480 | tf_op jit(solution)/shard_map/ppermute | solution.py:700
  111.3 2.8 project.1
  122.8 2.8 pad_maximum_fusion.gate_ref
  125.6 7.5 %collective-permute-done.13 = bf16[256,1024]{1,0:T(8,128)(2,1)S(1)} collective-permute-done((bf16[256,1024]{1,0:T(8,128)(2,1)S(1)}, bf16[256,1024]{1,0:T(8,128)(2,1)S(1)}, u32[]{:S(2)}, u32[]{:S(2)}) %collective-permute-start.13) | collective-permute-done | bytes 524320 | tf_op jit(solution)/shard_map/ppermute | solution.py:700
  134.0 3.4 collective-permute-start.20
  140.6 2.8 collective-permute-done.20
  149.7 7.7 %collective-permute-done.22 = bf16[256,1024]{1,0:T(8,128)(2,1)S(1)} collective-permute-done((bf16[256,1024]{1,0:T(8,128)(2,1)S(1)}, bf16[256,1024]{1,0:T(8,128)(2,1)S(1)}, u32[]{:S(2)}, u32[]{:S(2)}) %collective-permute-start.22) | collective-permute-done | bytes 524320 | tf_op jit(solution)/shard_map/ppermute | solution.py:700
  160.5 5.0 %collective-permute-done.27 = bf16[4,128,1024]{2,1,0:T(8,128)(2,1)} collective-permute-done((bf16[4,128,1024]{2,1,0:T(8,128)(2,1)}, bf16[4,128,1024]{2,1,0:T(8,128)(2,1)}, u32[]{:S(2)}, u32[]{:S(2)}) %collective-permute-start.27) | collective-permute-done | bytes 1048608 | tf_op jit(solution)/shard_map/ppermute | solution.py:700
  170.8 14.9 %collective-permute-done.28 = bf16[4,128,1024]{2,1,0:T(8,128)(2,1)} collective-permute-done((bf16[4,128,1024]{2,1,0:T(8,128)(2,1)}, bf16[4,128,1024]{2,1,0:T(8,128)(2,1)}, u32[]{:S(2)}, u32[]{:S(2)}) %collective-permute-start.28) | collective-permute-done | bytes 1048608 | tf_op jit(solution)/shard_map/ppermute | solution.py:700
  188.7 32.8 %experts.1 = (bf16[2048,1024]{1,0:T(8,128)(2,1)}, bf16[2048,1024]{1,0:T(8,128)(2,1)}, bf16[2048,1024]{1,0:T(8,128)(2,1)}, bf16[2048,16]{1,0:T(8,128)(2,1)}, f32[...) custom-call(s32[1]{0:T(128)} %bitcast.11.first, ...), custom_call_target="tpu_custom_call" | custom-call | tf_op jit(solution)/shard_map/experts/pallas_call | solution.py:315
  221.5 16.3 %back_rows.1 = (bf16[512,1024]{1,0:T(8,128)(2,1)}, bf16[512,1024]{1,0:T(8,128)(2,1)}, bf16[512,1024]{1,0:T(8,128)(2,1)}, bf16[512,1024]{1,0:T(8,128)(2,1)}) custom-call(bf16[2048,1024]{1,0:T(8,128)(2,1)} %get-tuple-element.158.gate_grad_ref.grad_ref, bf16[2048,1024]{1,0:T(8,128)(2,1)} %get-tuple-element.163.up_grad_ref.grad_ref, ...), custom_call_target="tpu_custom_call" | custom-call | tf_op jit(solution)/shard_map/back_rows/pallas_call | solution.py:371
  244.0 19.4 %collective-permute-done.63 = bf16[4,128,1024]{2,1,0:T(8,128)(2,1)S(1)} collective-permute-done((bf16[4,128,1024]{2,1,0:T(8,128)(2,1)S(1)}, bf16[4,128,1024]{2,1,0:T(8,128)(2,1)S(1)}, u32[]{:S(2)}, u32[]{:S(2)}) %collective-permute-start.63) | collective-permute-done | bytes 1048608 | tf_op jit(solution)/shard_map/ppermute | solution.py:700
  266.4 8.7 %weight_grads.2 = (bf16[4,128,1024]{2,1,0:T(8,128)(2,1)}, bf16[4,128,1024]{2,1,0:T(8,128)(2,1)}) custom-call(bf16[2048,1024]{1,0:T(8,128)(2,1)} %get-tuple-element.158.gate_grad_ref.grad_ref, bf16[512,1024]{1,0:T(8,128)(2,1)} %constant_dynamic-update-slice_fusion.9.h_0, bf16[512,1024]{1,0:T(8,128)(2,1)} %constant_dynamic-update-slice_fusion.11.h_1, ...), custom_call_target="tpu_custom_call" | custom-call | tf_op jit(solution)/shard_map/weight_grads/pallas_call | solution.py:407
  279.8 19.0 %collective-permute-done.61 = bf16[4,128,1024]{2,1,0:T(8,128)(2,1)S(1)} collective-permute-done((bf16[4,128,1024]{2,1,0:T(8,128)(2,1)}, bf16[4,128,1024]{2,1,0:T(8,128)(2,1)S(1)}, u32[]{:S(2)}, u32[]{:S(2)}) %collective-permute-start.61) | collective-permute-done | bytes 1048608 | tf_op jit(solution)/shard_map/ppermute | solution.py:700
  298.8 9.5 %expert_results.1 = (bf16[512,1024]{1,0:T(8,128)(2,1)}, bf16[512,1024]{1,0:T(8,128)(2,1)}, bf16[512,1024]{1,0:T(8,128)(2,1)}, bf16[512,1024]{1,0:T(8,128)(2,1)}) custom-call(bf16[2048,1024]{1,0:T(8,128)(2,1)} %get-tuple-element.121.act_ref, bf16[1024,1024]{1,0:T(8,128)(2,1)} %bitcast.72), custom_call_target="tpu_custom_call" | custom-call | tf_op jit(solution)/shard_map/expert_results/pallas_call | solution.py:432
  311.0 8.8 %weight_grads.3 = (bf16[4,128,1024]{2,1,0:T(8,128)(2,1)}, bf16[4,128,1024]{2,1,0:T(8,128)(2,1)}) custom-call(bf16[2048,1024]{1,0:T(8,128)(2,1)} %get-tuple-element.163.up_grad_ref.grad_ref, bf16[512,1024]{1,0:T(8,128)(2,1)} %constant_dynamic-update-slice_fusion.9.h_0, bf16[512,1024]{1,0:T(8,128)(2,1)} %constant_dynamic-update-slice_fusion.11.h_1, ...), custom_call_target="tpu_custom_call" | custom-call | tf_op jit(solution)/shard_map/weight_grads/pallas_call | solution.py:407
  323.9 3.3 out_grads.1
  331.9 19.9 %attend_back.1 = (bf16[4,144,512]{2,1,0:T(8,128)(2,1)}, bf16[4,144,512]{2,1,0:T(8,128)(2,1)}, bf16[256,1024]{1,0:T(8,128)(2,1)}, bf16[256,1024]{1,0:T(8,128)(2,1...) custom-call(s32[4]{0:T(128)} %fusion.35.blocks, s32[8]{0:T(128)} %fusion.37.shard_at, ...), custom_call_target="tpu_custom_call" | custom-call | tf_op jit(solution)/shard_map/attend_back/pallas_call | solution.py:608
  357.3 5.2 %collective-permute-done.54 = bf16[128,1024]{1,0:T(8,128)(2,1)} collective-permute-done((bf16[128,1024]{1,0:T(8,128)(2,1)}, bf16[128,1024]{1,0:T(8,128)(2,1)}, u32[]{:S(2)}, u32[]{:S(2)}) %collective-permute-start.54) | collective-permute-done | bytes 262176 | tf_op jit(solution)/shard_map/ppermute | solution.py:700
  366.9 7.3 %collective-permute-done.41 = bf16[4,144,512]{2,1,0:T(8,128)(2,1)} collective-permute-done((bf16[4,144,512]{2,1,0:T(8,128)(2,1)}, bf16[4,144,512]{2,1,0:T(8,128)(2,1)}, u32[]{:S(2)}, u32[]{:S(2)}) %collective-permute-start.41) | collective-permute-done | bytes 589856 | tf_op jit(solution)/shard_map/ppermute | solution.py:700
  385.5 11.8 %collective-permute-done.44 = bf16[144,512]{1,0:T(8,128)(2,1)S(1)} collective-permute-done((bf16[144,512]{1,0:T(8,128)(2,1)S(1)}, bf16[144,512]{1,0:T(8,128)(2,1)S(1)}, u32[]{:S(2)}, u32[]{:S(2)}) %collective-permute-start.44) | collective-permute-done | bytes 147488 | tf_op jit(solution)/shard_map/ppermute | solution.py:700
  400.2 3.2 collective-permute-start.48
  403.3 4.1 multiply_subtract_fusion.1
  427.0 4.2 multiply_subtract_fusion
  444.1 4.8 %qkv_step.1 = (f32[128,2048]{1,0:T(8,128)}, f32[128,2048]{1,0:T(8,128)}, f32[128,2048]{1,0:T(8,128)}, f32[16,512]{1,0:T(8,128)}) custom-call(s32[4]{0:T(128)} %fusion.38.slots, bf16[4,144,512]{2,1,0:T(8,128)(2,1)} %pad_maximum_fusion.6.g_ref, f32[128,2048]{1,0:T(8,128)} %w_ref.1, f32[128,2048]{1,0:T(8,128)} %m_ref.1, f32[128,2048]{1,0:T(8,128)} %v_ref.1), custom_call_target="tpu_custom_call" | custom-call | tf_op jit(solution)/shard_map/qkv_step/pallas_call | solution.py:686
  (376 shorter events, 153.4 us)
Async XLA Ops:
  7.2 79.4 %all-gather.8.cloned.1.call-start = ((), (), s32[]{:S(2)}) async-start(), calls=%async_computation.7 | async-start | bytes 1572864 | tf_op jit(solution)/shard_map/all_gather | solution.py:767
  10.1 91.9 %all-gather.10.cloned.1.call-start = ((), (), s32[]{:S(2)}) async-start(), calls=%async_computation.8 | async-start | bytes 1572864 | tf_op jit(solution)/shard_map/all_gather | solution.py:767
  10.8 134.1 %all-gather.6.cloned.1.call-start = ((), (), s32[]{:S(2)}) async-start(), calls=%async_computation.3 | async-start | bytes 1572864 | tf_op jit(solution)/shard_map/all_gather | solution.py:767
  10.9 59.1 %collective-permute-start = (bf16[256,1024]{1,0:T(8,128)(2,1)S(1)}, bf16[256,1024]{1,0:T(8,128)(2,1)}, u32[]{:S(2)}, u32[]{:S(2)}) collective-permute-start(bf16[256,1024]{1,0:T(8,128)(2,1)S(1)} %bitcast.69), channel_id=1, source_target_pairs={{0,16},{16,0},{1,17},{17,1},{2,18},{18,2},{3,19},{19,3},{4,20},{20... | collective-permute-start | bytes 1572872 | tf_op jit(solution)/shard_map/ppermute | solution.py:700
  12.5 74.2 %collective-permute-start.1 = (bf16[256,1024]{1,0:T(8,128)(2,1)S(1)}, bf16[256,1024]{1,0:T(8,128)(2,1)}, u32[]{:S(2)}, u32[]{:S(2)}) collective-permute-start(bf16[256,1024]{1,0:T(8,128)(2,1)S(1)} %bitcast.70), channel_id=1, source_target_pairs={{0,8},{8,0},{1,9},{9,1},{2,10},{10,2},{3,11},{11,3},{4,12},{12,4},... | collective-permute-start | bytes 1572872 | tf_op jit(solution)/shard_map/ppermute | solution.py:700
  15.5 27.6 %collective-permute-start.4 = (bf16[144,512]{1,0:T(8,128)(2,1)}, bf16[144,512]{1,0:T(8,128)(2,1)}, u32[]{:S(2)}, u32[]{:S(2)}) collective-permute-start(bf16[144,512]{1,0:T(8,128)(2,1)} %get-tuple-element.230), channel_id=1, source_target_pairs={{0,4},{2,6},{4,0},{6,2},{1,5},{3,7},{5,1},{7,3},{8,12},{10,14},{12... | collective-permute-start | bytes 442376 | tf_op jit(solution)/shard_map/ppermute | solution.py:700
  18.1 30.8 %collective-permute-start.3 = (bf16[144,512]{1,0:T(8,128)(2,1)}, bf16[144,512]{1,0:T(8,128)(2,1)}, u32[]{:S(2)}, u32[]{:S(2)}) collective-permute-start(bf16[144,512]{1,0:T(8,128)(2,1)} %get-tuple-element.230), channel_id=1, source_target_pairs={{0,2},{2,4},{4,6},{6,0},{1,3},{3,5},{5,7},{7,1},{8,10},{10,12},{12... | collective-permute-start | bytes 442376 | tf_op jit(solution)/shard_map/ppermute | solution.py:700
  21.4 381.9 %reduce-scatter.8.cloned.1.call-start = ((), (), s32[]{:S(2)}) async-start(), calls=%async_computation.6 | async-start | bytes 1572864 | tf_op jit(solution)/shard_map/reduce_scatter | solution.py:776
  71.1 37.8 %collective-permute-start.10 = (bf16[256,1024]{1,0:T(8,128)(2,1)S(1)}, bf16[256,1024]{1,0:T(8,128)(2,1)}, u32[]{:S(2)}, u32[]{:S(2)}) collective-permute-start(bf16[256,1024]{1,0:T(8,128)(2,1)S(1)} %pad_maximum_fusion.9), channel_id=1, source_target_pairs={{0,6},{10,8},{20,18},{30,28},{1,7},{11,9},{21,19},{31,29}} | collective-permute-start | bytes 1572872 | tf_op jit(solution)/shard_map/ppermute | solution.py:867
  81.6 27.4 %collective-permute-start.9 = (bf16[256,1024]{1,0:T(8,128)(2,1)S(1)}, bf16[256,1024]{1,0:T(8,128)(2,1)}, u32[]{:S(2)}, u32[]{:S(2)}) collective-permute-start(bf16[256,1024]{1,0:T(8,128)(2,1)S(1)} %pad_maximum_fusion.9), channel_id=1, source_target_pairs={{0,4},{10,14},{20,16},{30,26},{1,5},{11,15},{21,17},{31,27}} | collective-permute-start | bytes 1572872 | tf_op jit(solution)/shard_map/ppermute | solution.py:867
  83.1 26.0 %collective-permute-start.8 = (bf16[256,1024]{1,0:T(8,128)(2,1)S(1)}, bf16[256,1024]{1,0:T(8,128)(2,1)}, u32[]{:S(2)}, u32[]{:S(2)}) collective-permute-start(bf16[256,1024]{1,0:T(8,128)(2,1)S(1)} %pad_maximum_fusion.9), channel_id=1, source_target_pairs={{0,2},{10,12},{20,22},{30,24},{1,3},{11,13},{21,23},{31,25}} | collective-permute-start | bytes 1572872 | tf_op jit(solution)/shard_map/ppermute | solution.py:867
  86.6 36.1 %collective-permute-start.14 = (bf16[4,128,1024]{2,1,0:T(8,128)(2,1)}, bf16[4,128,1024]{2,1,0:T(8,128)(2,1)}, u32[]{:S(2)}, u32[]{:S(2)}) collective-permute-start(bf16[4,128,1024]{2,1,0:T(8,128)(2,1)} %bitcast.77), channel_id=1, source_target_pairs={{0,1},{1,0},{2,3},{3,2},{4,5},{5,4},{6,7},{7,6},{8,9},{9,8},{10,11... | collective-permute-start | bytes 3145736 | tf_op jit(solution)/shard_map/ppermute | solution.py:700
  139.1 26.4 %collective-permute-start.27 = (bf16[4,128,1024]{2,1,0:T(8,128)(2,1)}, bf16[4,128,1024]{2,1,0:T(8,128)(2,1)}, u32[]{:S(2)}, u32[]{:S(2)}) collective-permute-start(bf16[4,128,1024]{2,1,0:T(8,128)(2,1)} %bitcast.7), channel_id=1, source_target_pairs={{0,1},{1,0},{2,3},{3,2},{4,5},{5,4},{6,7},{7,6},{8,9},{9,8},{10,11... | collective-permute-start | bytes 3145736 | tf_op jit(solution)/shard_map/ppermute | solution.py:700
  147.5 39.5 %collective-permute-start.26 = (bf16[512,1152]{1,0:T(8,128)(2,1)}, bf16[512,1152]{1,0:T(8,128)(2,1)S(1)}, u32[]{:S(2)}, u32[]{:S(2)}) collective-permute-start(bf16[512,1152]{1,0:T(8,128)(2,1)} %constant_dynamic-update-slice_fusion.7.pack_1), channel_id=1, source_target_pairs={{0,8},{8,0},{1,9},{9,1},{2,10},{10,2},{3,11},{11,3},{4,12},{12,4},... | collective-permute-start | bytes 3538952 | tf_op jit(solution)/shard_map/ppermute | solution.py:700
  147.5 39.5 %collective-permute-start.25 = (bf16[512,1152]{1,0:T(8,128)(2,1)}, bf16[512,1152]{1,0:T(8,128)(2,1)}, u32[]{:S(2)}, u32[]{:S(2)}) collective-permute-start(bf16[512,1152]{1,0:T(8,128)(2,1)} %constant_dynamic-update-slice_fusion.5.pack_0), channel_id=1, source_target_pairs={{0,8},{8,0},{1,9},{9,1},{2,10},{10,2},{3,11},{11,3},{4,12},{12,4},... | collective-permute-start | bytes 3538952 | tf_op jit(solution)/shard_map/ppermute | solution.py:700
  157.4 28.3 %collective-permute-start.28 = (bf16[4,128,1024]{2,1,0:T(8,128)(2,1)}, bf16[4,128,1024]{2,1,0:T(8,128)(2,1)}, u32[]{:S(2)}, u32[]{:S(2)}) collective-permute-start(bf16[4,128,1024]{2,1,0:T(8,128)(2,1)} %all-gather.6.cloned.1.call-done), channel_id=1, source_target_pairs={{0,1},{1,0},{2,3},{3,2},{4,5},{5,4},{6,7},{7,6},{8,9},{9,8},{10,11... | collective-permute-start | bytes 3145736 | tf_op jit(solution)/shard_map/ppermute | solution.py:700
  159.7 27.4 %collective-permute-start.24 = (bf16[512,1024]{1,0:T(8,128)(2,1)}, bf16[512,1024]{1,0:T(8,128)(2,1)}, u32[]{:S(2)}, u32[]{:S(2)}) collective-permute-start(bf16[512,1024]{1,0:T(8,128)(2,1)} %constant_dynamic-update-slice_fusion.11.h_1), channel_id=1, source_target_pairs={{0,8},{8,0},{1,9},{9,1},{2,10},{10,2},{3,11},{11,3},{4,12},{12,4},... | collective-permute-start | bytes 3145736 | tf_op jit(solution)/shard_map/ppermute | solution.py:700
  165.5 21.5 %collective-permute-start.23 = (bf16[512,1024]{1,0:T(8,128)(2,1)}, bf16[512,1024]{1,0:T(8,128)(2,1)}, u32[]{:S(2)}, u32[]{:S(2)}) collective-permute-start(bf16[512,1024]{1,0:T(8,128)(2,1)} %constant_dynamic-update-slice_fusion.9.h_0), channel_id=1, source_target_pairs={{0,8},{8,0},{1,9},{9,1},{2,10},{10,2},{3,11},{11,3},{4,12},{12,4},... | collective-permute-start | bytes 3145736 | tf_op jit(solution)/shard_map/ppermute | solution.py:700
  238.3 25.1 %collective-permute-start.63 = (bf16[4,128,1024]{2,1,0:T(8,128)(2,1)S(1)}, bf16[4,128,1024]{2,1,0:T(8,128)(2,1)S(1)}, u32[]{:S(2)}, u32[]{:S(2)}) collective-permute-start(bf16[4,128,1024]{2,1,0:T(8,128)(2,1)S(1)} %copy-done.75), channel_id=1, source_target_pairs={{0,1},{1,0},{2,3},{3,2},{4,5},{5,4},{6,7},{7,6},{8,9},{9,8},{10,11... | collective-permute-start | bytes 3145736 | tf_op jit(solution)/shard_map/ppermute | solution.py:700
  266.3 160.6 %reduce-scatter.4.cloned.1.call-start = ((), (), s32[]{:S(2)}) async-start(), calls=%async_computation.4 | async-start | bytes 1572864 | tf_op jit(solution)/shard_map/reduce_scatter | solution.py:776
  275.1 23.8 %collective-permute-start.61 = (bf16[4,128,1024]{2,1,0:T(8,128)(2,1)}, bf16[4,128,1024]{2,1,0:T(8,128)(2,1)S(1)}, u32[]{:S(2)}, u32[]{:S(2)}) collective-permute-start(bf16[4,128,1024]{2,1,0:T(8,128)(2,1)} %get-tuple-element.160), channel_id=1, source_target_pairs={{0,1},{1,0},{2,3},{3,2},{4,5},{5,4},{6,7},{7,6},{8,9},{9,8},{10,11... | collective-permute-start | bytes 3145736 | tf_op jit(solution)/shard_map/ppermute | solution.py:700
  278.3 30.0 %collective-permute-start.35 = (bf16[256,1024]{1,0:T(8,128)(2,1)S(1)}, bf16[256,1024]{1,0:T(8,128)(2,1)S(1)}, u32[]{:S(2)}, u32[]{:S(2)}) collective-permute-start(bf16[256,1024]{1,0:T(8,128)(2,1)S(1)} %fusion.55.refs_0_), channel_id=1, source_target_pairs={{0,16},{16,0},{1,17},{17,1},{2,18},{18,2},{3,19},{19,3},{4,20},{20... | collective-permute-start | bytes 1572872 | tf_op jit(solution)/shard_map/ppermute | solution.py:700
  310.3 116.6 %reduce-scatter.6.cloned.1.call-start = ((), (), s32[]{:S(2)}) async-start(), calls=%async_computation.5 | async-start | bytes 1572864 | tf_op jit(solution)/shard_map/reduce_scatter | solution.py:776
  319.8 33.2 %collective-permute-start.62 = (bf16[4,128,1024]{2,1,0:T(8,128)(2,1)}, bf16[4,128,1024]{2,1,0:T(8,128)(2,1)S(1)}, u32[]{:S(2)}, u32[]{:S(2)}) collective-permute-start(bf16[4,128,1024]{2,1,0:T(8,128)(2,1)} %get-tuple-element.165), channel_id=1, source_target_pairs={{0,1},{1,0},{2,3},{3,2},{4,5},{5,4},{6,7},{7,6},{8,9},{9,8},{10,11... | collective-permute-start | bytes 3145736 | tf_op jit(solution)/shard_map/ppermute | solution.py:700
  375.5 21.8 %collective-permute-start.44 = (bf16[144,512]{1,0:T(8,128)(2,1)S(1)}, bf16[144,512]{1,0:T(8,128)(2,1)S(1)}, u32[]{:S(2)}, u32[]{:S(2)}) collective-permute-start(bf16[144,512]{1,0:T(8,128)(2,1)S(1)} %get-tuple-element.237), channel_id=1, source_target_pairs={{0,6},{2,0},{4,2},{6,4},{1,7},{3,1},{5,3},{7,5},{8,14},{10,8},{12,... | collective-permute-start | bytes 442376 | tf_op jit(solution)/shard_map/ppermute | solution.py:700
  377.4 21.4 %collective-permute-start.46 = (bf16[144,512]{1,0:T(8,128)(2,1)S(1)}, bf16[144,512]{1,0:T(8,128)(2,1)S(1)}, u32[]{:S(2)}, u32[]{:S(2)}) collective-permute-start(bf16[144,512]{1,0:T(8,128)(2,1)S(1)} %get-tuple-element.238), channel_id=1, source_target_pairs={{0,2},{2,4},{4,6},{6,0},{1,3},{3,5},{5,7},{7,1},{8,10},{10,12},{12... | collective-permute-start | bytes 442376 | tf_op jit(solution)/shard_map/ppermute | solution.py:700
  377.6 21.4 %collective-permute-start.45 = (bf16[144,512]{1,0:T(8,128)(2,1)S(1)}, bf16[144,512]{1,0:T(8,128)(2,1)S(1)}, u32[]{:S(2)}, u32[]{:S(2)}) collective-permute-start(bf16[144,512]{1,0:T(8,128)(2,1)S(1)} %get-tuple-element.239), channel_id=1, source_target_pairs={{0,4},{2,6},{4,0},{6,2},{1,5},{3,7},{5,1},{7,3},{8,12},{10,14},{12... | collective-permute-start | bytes 442376 | tf_op jit(solution)/shard_map/ppermute | solution.py:700
  381.9 26.6 %collective-permute-start.57 = (bf16[128,1024]{1,0:T(8,128)(2,1)}, bf16[128,1024]{1,0:T(8,128)(2,1)}, u32[]{:S(2)}, u32[]{:S(2)}) collective-permute-start(bf16[128,1024]{1,0:T(8,128)(2,1)} %add_convert_fusion.20), channel_id=1, source_target_pairs={{6,0},{8,10},{18,20},{28,30},{7,1},{9,11},{19,21},{29,31}} | collective-permute-start | bytes 786440 | tf_op jit(solution)/shard_map/ppermute | solution.py:961
  383.3 25.7 %collective-permute-start.56 = (bf16[128,1024]{1,0:T(8,128)(2,1)}, bf16[128,1024]{1,0:T(8,128)(2,1)}, u32[]{:S(2)}, u32[]{:S(2)}) collective-permute-start(bf16[128,1024]{1,0:T(8,128)(2,1)} %add_convert_fusion.20), channel_id=1, source_target_pairs={{4,0},{14,10},{16,20},{26,30},{5,1},{15,11},{17,21},{27,31}} | collective-permute-start | bytes 786440 | tf_op jit(solution)/shard_map/ppermute | solution.py:961
  413.3 25.5 %collective-permute-start.60 = (bf16[128,1024]{1,0:T(8,128)(2,1)}, bf16[128,1024]{1,0:T(8,128)(2,1)}, u32[]{:S(2)}, u32[]{:S(2)}) collective-permute-start(bf16[128,1024]{1,0:T(8,128)(2,1)} %add_convert_fusion.19), channel_id=1, source_target_pairs={{0,24},{10,2},{20,12},{30,22},{1,25},{11,3},{21,13},{31,23}} | collective-permute-start | bytes 786440 | tf_op jit(solution)/shard_map/ppermute | solution.py:972
  414.7 24.6 %collective-permute-start.59 = (bf16[128,1024]{1,0:T(8,128)(2,1)}, bf16[128,1024]{1,0:T(8,128)(2,1)}, u32[]{:S(2)}, u32[]{:S(2)}) collective-permute-start(bf16[128,1024]{1,0:T(8,128)(2,1)} %add_convert_fusion.19), channel_id=1, source_target_pairs={{0,16},{10,26},{20,4},{30,14},{1,17},{11,27},{21,5},{31,15}} | collective-permute-start | bytes 786440 | tf_op jit(solution)/shard_map/ppermute | solution.py:972
  416.4 23.0 %collective-permute-start.58 = (bf16[128,1024]{1,0:T(8,128)(2,1)}, bf16[128,1024]{1,0:T(8,128)(2,1)}, u32[]{:S(2)}, u32[]{:S(2)}) collective-permute-start(bf16[128,1024]{1,0:T(8,128)(2,1)} %add_convert_fusion.19), channel_id=1, source_target_pairs={{0,8},{10,18},{20,28},{30,6},{1,9},{11,19},{21,29},{31,7}} | collective-permute-start | bytes 786440 | tf_op jit(solution)/shard_map/ppermute | solution.py:972
  (114 other events, 1607.2 us)
Sparse Core Ops, SparseCore 0:
  10.2 43.5 all-gather.7
  56.0 45.6 all-gather.9
  103.8 32.9 all-gather.5
  266.5 27.6 reduce-scatter.7
  310.4 27.8 reduce-scatter.3
  356.5 39.5 reduce-scatter.5
where the time goes:
time: 467 us; the launch traced here: 461 us
  waiting for transfers between devices  151 us (32%)
  Pallas kernels  121 us (26%)
  starting transfers between devices  69.1 us (15%)
  other arithmetic  65.5 us (14%)
  local copies, waits for them, and re-layouts  39.3 us (8%)
  between operations  15.5 us (3%)
    ppermute x55, waiting for transfers between devices, shifted(): lax.ppermute(value, axis, [(j, (j + step) % size) for j in range(size)])  148 us
    ppermute x55, starting transfers between devices, shifted(): lax.ppermute(value, axis, [(j, (j + step) % size) for j in range(size)])  56 us
    pallas_call x1, Pallas kernels, run_experts(): pl.pallas_call(experts_kernel, grid=(len(h_all),), out_shape=(jax.ShapeDt...  32.8 us
    convert_element_type x22, other arithmetic, give_back(): return total.astype(low)  24.1 us
    unnamed x164, local copies, waits for them, and re-layouts  23.1 us
    pallas_call x1, Pallas kernels, attend_back(): pl.pallas_call(functools.partial(attend_back_kernel, count, heads, keys,...  19.9 us
    pallas_call x2, Pallas kernels, weight_grads(): pl.pallas_call(weight_grads_kernel, grid=(owned,), out_shape=(jax.ShapeDt...  17.5 us
    pallas_call x1, Pallas kernels, back_rows(): pl.pallas_call(back_rows_kernel, grid=(4,), out_shape=(jax.ShapeDtypeStru...  16.3 us
  transfers between devices with their start and end apart: 70, of which 21 were waited for; matrix products, arithmetic and copies ran while one was open for 20% of the time, Pallas kernels for 16%

commit v1 on v0

--- a/solution.py
+++ b/solution.py
@@ -695,6 +695,38 @@
     )(slots, grads, weight, first, second)
 
 
+def in_step_kernel(rate, gate_ref, up_ref, w_ref, m_ref, v_ref, m_out, v_out, w_out):
+    for index, grad_ref in enumerate((gate_ref, up_ref)):
+        first, second, weight = adam_step(
+            w_ref[0, index],
+            m_ref[0, index],
+            v_ref[0, index],
+            grad_ref[0].astype(high),
+            rate,
+            weight_decay,
+        )
+        m_out[0, index] = first
+        v_out[0, index] = second
+        w_out[0, index] = weight
+
+
+def in_step(rate, gate_grad, up_grad, weight, first, second):
+    like = jax.ShapeDtypeStruct(weight.shape, high)
+    owned, _, part, width = weight.shape
+    half = pl.BlockSpec((1, part, width), lambda i: (i, 0, 0))
+    block = pl.BlockSpec((1, 2, part, width), lambda i: (i, 0, 0, 0))
+    return pl.pallas_call(
+        functools.partial(in_step_kernel, rate),
+        grid=(owned,),
+        out_shape=(like, like, like),
+        in_specs=[half, half, block, block, block],
+        out_specs=(block, block, block),
+        compiler_params=PARAMS,
+        cost_estimate=NO_COST,
+        name="in_step",
+    )(gate_grad, up_grad, weight, first, second)
+
+
 def shifted(value, axis, step):
     size = lax.axis_size(axis)
     return lax.ppermute(value, axis, [(j, (j + step) % size) for j in range(size)])
@@ -721,21 +753,21 @@
 
 def collect_first(value):
     half = value.shape[0] // 2
-    return collect_rows(value[:half], "x"), collect_rows(value[half:], "near")
+    return collect_rows(value[:half], "x"), collect_rows(value[half:], "y")
 
 
 def collect_second(upper, lower):
-    return collect_rows(upper, "near"), collect_rows(lower, "x")
+    return collect_rows(upper, "y"), collect_rows(lower, "x")
 
 
 def collect_core(upper, lower):
     return [upper, lower, shifted(upper, "core", 1), shifted(lower, "core", 1)]
 
 
-def give_back_chip(pieces):
+def give_back_chip(pieces, others=()):
     return (
-        give_back([pieces[0], pieces[2]], "core"),
-        give_back([pieces[1], pieces[3]], "core"),
+        give_back([pieces[0], pieces[2]], "core", others),
+        give_back([pieces[1], pieces[3]], "core", others),
     )
 
 
@@ -743,13 +775,13 @@
     return give_back(rows.reshape(lax.axis_size(axis), -1, rows.shape[-1]), axis, others)
 
 
-def give_back_first(upper, lower):
-    return give_back_rows(upper, "near"), give_back_rows(lower, "x")
+def give_back_first(upper, lower, others=()):
+    return give_back_rows(upper, "y", others), give_back_rows(lower, "x", others)
 
 
 def give_back_second(upper, lower):
     return jnp.concatenate(
-        [give_back_rows(upper, "x"), give_back_rows(lower, "near")], axis=0
+        [give_back_rows(upper, "x"), give_back_rows(lower, "y")], axis=0
     )
 
 
@@ -763,17 +795,12 @@
     return [give_back([pieces[step], pieces[half + step]], "core") for step in range(half)]
 
 
-def collect_deep(shard):
-    return lax.all_gather(shard.astype(low), "far", axis=1, tiled=True)
-
-
 def collect_weight(shard):
-    return jnp.concatenate(collect(shard, "y"), axis=1)
-
-
-def give_back_weight(units, *others):
-    total = give_back(units, "y", others)
-    return lax.psum_scatter(total, "far", scatter_dimension=1, tiled=True)
+    return lax.all_gather(shard.astype(low), DEEP, axis=1, tiled=True)
+
+
+def give_back_weight(grad):
+    return lax.psum_scatter(grad, DEEP, scatter_dimension=1, tiled=True)
 
 
 def diagonal_moves(to_expert):
@@ -866,10 +893,9 @@
     for moves in diagonal_moves(False):
         out_all = out_all + lax.ppermute(out_pair, joint, moves)
     out_all = out_all.reshape(sides, part, width)
-    gate_deep = collect_deep(expert_in[:, 0])
-    up_deep = collect_deep(expert_in[:, 1])
-    down_deep = collect_deep(expert_out)
-    gate_w = collect_weight(gate_deep)
+    gate_w = collect_weight(expert_in[:, 0])
+    up_w = collect_weight(expert_in[:, 1])
+    down_w = collect_weight(expert_out)
     hidden = gate_w.shape[1]
     inner = owned * hidden
     chosen = jnp.any(
@@ -879,7 +905,6 @@
         after(jnp.concatenate([cotangent[0], chosen.astype(low)], axis=1), w_all)
     )
 
-    x_all[0] = after(x_all[0], gate_deep)
     normed, weight, extra, query, key, value, attended, totals = attend(
         blocks, shards, x_all, w_all, cosine, sine, heads, keys
     )
@@ -887,36 +912,33 @@
     gains_all = extra[EXTRA : EXTRA + 2].astype(high)
     gain_one = gains_all[0]
     gain_two = gains_all[1]
-    attended, up_deep = lax.optimization_barrier((attended, up_deep))
+    attended = after(attended, gate_w)
     pack = collect_second(*lax.optimization_barrier((*pack, attended))[:2])
     branch = give_back(
         give_back_core(project(blocks, side_slots, attended, out_all, spread)), "x"
     )
     inputs = tokens[0].astype(high)
-    middle = inputs + after(branch, gate_w, *pack).astype(high)
+    middle = inputs + after(branch, *pack).astype(high)
     scale_two = rms_scale(middle)
     norm_two = (middle * scale_two * gain_two).astype(low)
-    up_w = collect_weight(up_deep)
-    h_first = lax.optimization_barrier((*collect_first(norm_two), down_deep))
-    down_w = collect_weight(h_first[2])
+    h_first = lax.optimization_barrier((*collect_first(norm_two), up_w))
     h_all = collect_core(*collect_second(*h_first[:2]))
     pack_all = collect_core(*pack)
 
     first = (own * owned).astype(jnp.int32).reshape(1)
     act, gate_grad, up_grad, logit_grad, router_grad, *down_units = run_experts(
-        first, h_all, pack_all, router, gate_w, up_w, down_w, sides
+        first, h_all, pack_all, router, gate_w, up_w, down_w, 1
     )
     flat_gate = gate_w.reshape(inner, width)
     flat_up = up_w.reshape(inner, width)
     rows_grad = back_rows(gate_grad, up_grad, logit_grad, flat_gate, flat_up, router)
-    down_total = give_back_weight(down_units, *rows_grad)
-    gate_units = weight_grads(after(gate_grad, *rows_grad), h_all, owned, sides)
-    chip_grads = give_back_chip(rows_grad)
-    up_units = weight_grads(after(up_grad, gate_units[0], *chip_grads), h_all, owned, sides)
-    first_grads = give_back_first(*chip_grads)
-    gate_total = give_back_weight(gate_units, *first_grads)
-    norm_two_low = give_back_second(*first_grads)
-    up_total = give_back_weight(up_units, norm_two_low)
+    down_total = give_back_weight(down_units[0])
+    (gate_units,) = weight_grads(after(gate_grad, *rows_grad), h_all, owned, 1)
+    gate_total = give_back_weight(gate_units)
+    chip_grads = give_back_chip(rows_grad, (gate_units,))
+    (up_units,) = weight_grads(after(up_grad, gate_units, *chip_grads), h_all, owned, 1)
+    up_total = give_back_weight(up_units)
+    norm_two_low = give_back_second(*give_back_first(*chip_grads, (up_units,)))
     norm_two_grad = norm_two_low.astype(high)
     results = expert_results(after(act, norm_two_low), down_w.reshape(inner, width))
 
@@ -928,7 +950,10 @@
     results = lax.optimization_barrier((*results, grad_all[1]))[:4]
     mixed = give_back_chip(results)
     out_units = out_grads(blocks, side_slots, grad_all, attended)
-    grad_all[0] = after(grad_all[0], out_units[0], *mixed)
+    down_new = adam_step(
+        expert_out, down_m, down_v, down_total.astype(high), 3.0 * (FF // 16) ** (-0.5), weight_decay
+    )
+    grad_all[0] = after(grad_all[0], out_units[0], *mixed, down_new[0])
     qkv_grad, norm_one_grad = attend_back(
         blocks,
         shard_at,
@@ -952,7 +977,7 @@
     out_piece = give_back(out_units, "y", qkv_grad)
     norm_one_core = give_back_core(norm_one_grad)
     qkv_total = give_back(after(qkv_sum, *norm_one_core), DEEP)
-    upper = give_back_rows(mixed[0], "near", (qkv_total,))
+    upper = give_back_rows(mixed[0], "y", (qkv_total,))
     lower = give_back_rows(mixed[1], "x", (qkv_total,))
     norm_one_low = give_back(norm_one_core, "x", (qkv_total,))
     scale_one = rms_scale(inputs)
@@ -965,12 +990,13 @@
     input_grad = middle_grad + norm_back(inputs, scale_one, gain_one, norm_one_grad)
     mixed = give_back_second(upper, lower)
     output = (middle + mixed.astype(high)).astype(low)
+    qkv_total, gate_total = lax.optimization_barrier((qkv_total, gate_total))
     qkv_pieces = collect_expert(qkv_total)
     qkv_total = jnp.stack(qkv_pieces)
     out_total = jnp.where(at_z == own, out_piece, jnp.zeros_like(out_piece))
     for moves in diagonal_moves(True):
         out_total = out_total + lax.ppermute(out_piece, joint, moves)
-    gate_total = after(gate_total, qkv_pieces[1])
+    gate_total, up_total = lax.optimization_barrier((gate_total, up_total, *qkv_pieces[1:]))[:2]
 
     rate = 3.0 * D ** (-0.5)
     qkv_new_m, qkv_new_v, qkv_new_w, extra_total = qkv_step(
@@ -978,21 +1004,14 @@
     )
     router_total = extra_total[:experts, :part].T
     gains_total = extra_total[:2, part : 2 * part]
-    in_total = jnp.stack([gate_total, up_total], axis=1)
-    rates = (
-        3.0 * (HQ * HD * 8 // length) ** (-0.5),
-        3.0 * (4 * D) ** (-0.5),
-        0.6,
-        rate,
-        3.0 * (FF // 16) ** (-0.5),
-    )
-    decays = (weight_decay, weight_decay, 0.0, weight_decay, weight_decay)
-    masters = (out_w, router_w, gains, expert_in, expert_out)
-    firsts = (out_m, router_m, gains_m, in_m, down_m)
-    seconds = (out_v, router_v, gains_v, in_v, down_v)
-    grads = (out_total, router_total, gains_total, in_total, down_total)
+    rates = (3.0 * (HQ * HD * 8 // length) ** (-0.5), 3.0 * (4 * D) ** (-0.5), 0.6)
+    decays = (weight_decay, weight_decay, 0.0)
+    masters = (out_w, router_w, gains)
+    firsts = (out_m, router_m, gains_m)
+    seconds = (out_v, router_v, gains_v)
+    grads = (out_total, router_total, gains_total)
     updated = [qkv_new_m, qkv_new_v, qkv_new_w]
-    for index in range(5):
+    for index in range(3):
         updated.extend(
             adam_step(
                 masters[index],
@@ -1003,6 +1022,8 @@
                 decays[index],
             )
         )
+    updated.extend(in_step(rate, gate_total, up_total, expert_in, in_m, in_v))
+    updated.extend(down_new)
     return (output[None], input_grad[None], *updated)
 
 

time: 467 us -> 463 us (level)
  waiting for transfers between devices: 151 us -> 179 us
  local copies, waits for them, and re-layouts: 39.3 us -> 22.5 us
  other arithmetic: 65.5 us -> 50.7 us
  starting transfers between devices: 69.1 us -> 60.1 us
  Pallas kernels: 121 us -> 127 us
    ppermute x3, waiting for transfers between devices: 0.01 us -> 27.4 us  [body(): out_all = out_all + lax.ppermute(out_pair, joint, moves)]
    unnamed x164 -> x139, local copies, waits for them, and re-layouts: 23.1 us -> 9.49 us
    convert_element_type x22 -> x19, other arithmetic: 24.1 us -> 16.5 us  [give_back(): return total.astype(low)]
    ppermute x55 -> x49, starting transfers between devices: 56 us -> 48.8 us  [shifted(): lax.ppermute(value, axis, [(j, (j + step) % size) for j in range(size)])]
    pallas_call x0 -> x1, Pallas kernels: none -> 6.55 us  [in_step(): pl.pallas_call(functools.partial(in_step_kernel, rate), grid=(owned,), ou...]
    sub x5 -> x4, other arithmetic: 13.5 us -> 9.85 us  [adam_step(): return (new_first, new_second, weight - rate * (update + decay * weight))]
    ppermute x55 -> x49, waiting for transfers between devices: 148 us -> 150 us  [shifted(): lax.ppermute(value, axis, [(j, (j + step) % size) for j in range(size)])]
  transfers between devices with their start and end apart: 70 -> 64, of which waited for: 21 -> 27; matrix products, arithmetic and copies ran while one was open for 20% -> 14% of each run, Pallas kernels for 16% -> 19%
where the time goes in v1:
time: 463 us; the launch traced here: 455 us
  waiting for transfers between devices  179 us (39%)
  Pallas kernels  127 us (27%)
  starting transfers between devices  60.1 us (13%)
  other arithmetic  50.7 us (11%)
  local copies, waits for them, and re-layouts  22.5 us (5%)
  between operations  15.4 us (3%)
    ppermute x49, waiting for transfers between devices, shifted(): lax.ppermute(value, axis, [(j, (j + step) % size) for j in range(size)])  150 us
    ppermute x49, starting transfers between devices, shifted(): lax.ppermute(value, axis, [(j, (j + step) % size) for j in range(size)])  48.8 us
    pallas_call x1, Pallas kernels, run_experts(): pl.pallas_call(experts_kernel, grid=(len(h_all),), out_shape=(jax.ShapeDt...  32.4 us
    ppermute x3, waiting for transfers between devices, body(): out_all = out_all + lax.ppermute(out_pair, joint, moves)  27.4 us
    pallas_call x1, Pallas kernels, attend_back(): pl.pallas_call(functools.partial(attend_back_kernel, count, heads, keys,...  19.5 us
    pallas_call x2, Pallas kernels, weight_grads(): pl.pallas_call(weight_grads_kernel, grid=(owned,), out_shape=(jax.ShapeDt...  17.4 us
    pallas_call x1, Pallas kernels, back_rows(): pl.pallas_call(back_rows_kernel, grid=(4,), out_shape=(jax.ShapeDtypeStru...  16.6 us
    convert_element_type x19, other arithmetic, give_back(): return total.astype(low)  16.5 us
  transfers between devices with their start and end apart: 64, of which 27 were waited for; matrix products, arithmetic and copies ran while one was open for 14% of the time, Pallas kernels for 19%

profile of v1, /device:TPU:8, one launch (start us, length us, event | category | flops | bytes accessed | tf_op | source)
XLA Modules:
  0.0 454.9 jit_solution(1263730714355349285)
XLA Ops:
  7.3 2.7 fusion.62
  25.6 15.6 %collective-permute-done.4 = bf16[144,512]{1,0:T(8,128)(2,1)S(1)} collective-permute-done((bf16[144,512]{1,0:T(8,128)(2,1)}, bf16[144,512]{1,0:T(8,128)(2,1)S(1)}, u32[]{:S(2)}, u32[]{:S(2)}) %collective-permute-start.4) | collective-permute-done | bytes 147488 | tf_op jit(solution)/shard_map/ppermute | solution.py:732
  41.2 6.8 %collective-permute-done.5 = bf16[144,512]{1,0:T(8,128)(2,1)} collective-permute-done((bf16[144,512]{1,0:T(8,128)(2,1)}, bf16[144,512]{1,0:T(8,128)(2,1)}, u32[]{:S(2)}, u32[]{:S(2)}) %collective-permute-start.5) | collective-permute-done | bytes 147488 | tf_op jit(solution)/shard_map/ppermute | solution.py:732
  52.1 13.2 %collective-permute-done.6 = bf16[4,144,512]{2,1,0:T(8,128)(2,1)S(1)} collective-permute-done((bf16[4,144,512]{2,1,0:T(8,128)(2,1)S(1)}, bf16[4,144,512]{2,1,0:T(8,128)(2,1)S(1)}, u32[]{:S(2)}, u32[]{:S(2)}) %collective-permute-start.6) | collective-permute-done | bytes 589856 | tf_op jit(solution)/shard_map/ppermute | solution.py:732
  80.0 13.9 %attend.1 = (bf16[1024,1024]{1,0:T(8,128)(2,1)}, bf16[1024,512]{1,0:T(8,128)(2,1)}, bf16[32,1024]{1,0:T(8,128)(2,1)}, bf16[4,1024,64]{2,1,0:T(8,128)(2,1)}, bf16...) custom-call(s32[4]{0:T(128)} %fusion.33.blocks, ...), custom_call_target="tpu_custom_call" | custom-call | tf_op jit(solution)/shard_map/attend/pallas_call | solution.py:171
  94.0 27.3 %collective-permute-done.8 = bf16[256,1024]{1,0:T(8,128)(2,1)} collective-permute-done((bf16[256,1024]{1,0:T(8,128)(2,1)S(1)}, bf16[256,1024]{1,0:T(8,128)(2,1)}, u32[]{:S(2)}, u32[]{:S(2)}) %collective-permute-start.8) | collective-permute-done | bytes 524320 | tf_op jit(solution)/shard_map/ppermute | solution.py:894
  123.6 2.8 project.1
  126.4 8.7 %collective-permute-start.12 = (bf16[256,1024]{1,0:T(8,128)(2,1)}, bf16[256,1024]{1,0:T(8,128)(2,1)S(1)}, u32[]{:S(2)}, u32[]{:S(2)}) collective-permute-start(bf16[256,1024]{1,0:T(8,128)(2,1)} %get-tuple-element.101), channel_id=1, source_target_pairs={{0,8},{8,0},{1,9},{9,1},{2,10},{10,2},{3,11},{11,3},{4,12},{12,4},... | collective-permute-start | bytes 1572872 | tf_op jit(solution)/shard_map/ppermute | solution.py:732
  141.2 10.3 %collective-permute-done.16 = bf16[256,1152]{1,0:T(8,128)(2,1)S(1)} collective-permute-done((bf16[256,1152]{1,0:T(8,128)(2,1)S(1)}, bf16[256,1152]{1,0:T(8,128)(2,1)S(1)}, u32[]{:S(2)}, u32[]{:S(2)}) %collective-permute-start.16) | collective-permute-done | bytes 589856 | tf_op jit(solution)/shard_map/ppermute | solution.py:732
  155.1 9.7 %collective-permute-done.13 = bf16[256,1024]{1,0:T(8,128)(2,1)S(1)} collective-permute-done((bf16[256,1024]{1,0:T(8,128)(2,1)S(1)}, bf16[256,1024]{1,0:T(8,128)(2,1)S(1)}, u32[]{:S(2)}, u32[]{:S(2)}) %collective-permute-start.13) | collective-permute-done | bytes 524320 | tf_op jit(solution)/shard_map/ppermute | solution.py:732
  167.1 6.8 %collective-permute-done.18 = bf16[128,1024]{1,0:T(8,128)(2,1)S(1)} collective-permute-done((bf16[128,1024]{1,0:T(8,128)(2,1)S(1)}, bf16[128,1024]{1,0:T(8,128)(2,1)S(1)}, u32[]{:S(2)}, u32[]{:S(2)}) %collective-permute-start.18) | collective-permute-done | bytes 262176 | tf_op jit(solution)/shard_map/ppermute | solution.py:732
  179.7 8.6 %collective-permute-done.20 = bf16[256,1024]{1,0:T(8,128)(2,1)S(1)} collective-permute-done((bf16[256,1024]{1,0:T(8,128)(2,1)}, bf16[256,1024]{1,0:T(8,128)(2,1)S(1)}, u32[]{:S(2)}, u32[]{:S(2)}) %collective-permute-start.20) | collective-permute-done | bytes 524320 | tf_op jit(solution)/shard_map/ppermute | solution.py:732
  192.7 32.4 %experts.1 = (bf16[2048,1024]{1,0:T(8,128)(2,1)}, bf16[2048,1024]{1,0:T(8,128)(2,1)}, bf16[2048,1024]{1,0:T(8,128)(2,1)}, bf16[2048,16]{1,0:T(8,128)(2,1)}, f32[...) custom-call(s32[1]{0:T(128)} %bitcast.10.first, bf16[512,1024]{1,0:T(8,128)(2,1)} %copy-done.4, ...), custom_call_target="tpu_custom_call" | custom-call | tf_op jit(solution)/shard_map/experts/pallas_call | solution.py:315
  225.1 16.6 %back_rows.1 = (bf16[512,1024]{1,0:T(8,128)(2,1)}, bf16[512,1024]{1,0:T(8,128)(2,1)}, bf16[512,1024]{1,0:T(8,128)(2,1)}, bf16[512,1024]{1,0:T(8,128)(2,1)}) custom-call(bf16[2048,1024]{1,0:T(8,128)(2,1)} %get-tuple-element.117.gate_grad_ref.grad_ref, bf16[2048,1024]{1,0:T(8,128)(2,1)} %get-tuple-element.120.up_grad_ref.grad_ref, ...), custom_call_target="tpu_custom_call" | custom-call | tf_op jit(solution)/shard_map/back_rows/pallas_call | solution.py:371
  242.3 8.7 %weight_grads.2 = bf16[4,256,1024]{2,1,0:T(8,128)(2,1)} custom-call(bf16[2048,1024]{1,0:T(8,128)(2,1)} %get-tuple-element.117.gate_grad_ref.grad_ref, bf16[512,1024]{1,0:T(8,128)(2,1)} %copy-done.4, bf16[512,1024]{1,0:T(8,128)(2,1)} %copy-done.3, bf16[512,1024]{1,0:T(8,128)(2,1)} %collective-permute-done.22.h_2, bf16[512,1024]{1,0:T(8,128)(2,1)} %collective-permute-done.23.h_3), custom_call_target="tpu_custom_call" | custom-call | tf_op jit(solution)/shard_map/weight_grads/pallas_call | solution.py:407
  257.5 8.6 %weight_grads.3 = bf16[4,256,1024]{2,1,0:T(8,128)(2,1)} custom-call(bf16[2048,1024]{1,0:T(8,128)(2,1)} %get-tuple-element.120.up_grad_ref.grad_ref, bf16[512,1024]{1,0:T(8,128)(2,1)} %copy-done.4, bf16[512,1024]{1,0:T(8,128)(2,1)} %copy-done.3, bf16[512,1024]{1,0:T(8,128)(2,1)} %collective-permute-done.22.h_2, bf16[512,1024]{1,0:T(8,128)(2,1)} %collective-permute-done.23.h_3), custom_call_target="tpu_custom_call" | custom-call | tf_op jit(solution)/shard_map/weight_grads/pallas_call | solution.py:407
  276.6 3.7 collective-permute-done.29
  283.1 9.6 %expert_results.1 = (bf16[512,1024]{1,0:T(8,128)(2,1)}, bf16[512,1024]{1,0:T(8,128)(2,1)}, bf16[512,1024]{1,0:T(8,128)(2,1)}, bf16[512,1024]{1,0:T(8,128)(2,1)}) custom-call(bf16[2048,1024]{1,0:T(8,128)(2,1)} %get-tuple-element.123.act_ref, bf16[1024,1024]{1,0:T(8,128)(2,1)} %bitcast.69), custom_call_target="tpu_custom_call" | custom-call | tf_op jit(solution)/shard_map/expert_results/pallas_call | solution.py:432
  300.9 3.3 out_grads.1
  306.8 4.3 multiply_subtract_fusion
  311.1 19.5 %attend_back.1 = (bf16[4,144,512]{2,1,0:T(8,128)(2,1)}, bf16[4,144,512]{2,1,0:T(8,128)(2,1)}, bf16[256,1024]{1,0:T(8,128)(2,1)}, bf16[256,1024]{1,0:T(8,128)(2,1...) custom-call(s32[4]{0:T(128)} %fusion.33.blocks, s32[8]{0:T(128)} %fusion.35.shard_at, ...), custom_call_target="tpu_custom_call" | custom-call | tf_op jit(solution)/shard_map/attend_back/pallas_call | solution.py:608
  335.2 5.0 %collective-permute-done.51 = bf16[128,1024]{1,0:T(8,128)(2,1)} collective-permute-done((bf16[128,1024]{1,0:T(8,128)(2,1)}, bf16[128,1024]{1,0:T(8,128)(2,1)}, u32[]{:S(2)}, u32[]{:S(2)}) %collective-permute-start.51) | collective-permute-done | bytes 262176 | tf_op jit(solution)/shard_map/ppermute | solution.py:732
  342.6 10.3 %collective-permute-done.38 = bf16[4,144,512]{2,1,0:T(8,128)(2,1)} collective-permute-done((bf16[4,144,512]{2,1,0:T(8,128)(2,1)}, bf16[4,144,512]{2,1,0:T(8,128)(2,1)}, u32[]{:S(2)}, u32[]{:S(2)}) %collective-permute-start.38) | collective-permute-done | bytes 589856 | tf_op jit(solution)/shard_map/ppermute | solution.py:732
  355.6 4.5 collective-permute-start.42
  361.2 6.9 %collective-permute-done.43 = bf16[144,512]{1,0:T(8,128)(2,1)S(1)} collective-permute-done((bf16[144,512]{1,0:T(8,128)(2,1)S(1)}, bf16[144,512]{1,0:T(8,128)(2,1)S(1)}, u32[]{:S(2)}, u32[]{:S(2)}) %collective-permute-start.43) | collective-permute-done | bytes 147488 | tf_op jit(solution)/shard_map/ppermute | solution.py:732
  368.9 12.5 %collective-permute-done.42 = bf16[144,512]{1,0:T(8,128)(2,1)S(1)} collective-permute-done((bf16[144,512]{1,0:T(8,128)(2,1)S(1)}, bf16[144,512]{1,0:T(8,128)(2,1)S(1)}, u32[]{:S(2)}, u32[]{:S(2)}) %collective-permute-start.42) | collective-permute-done | bytes 147488 | tf_op jit(solution)/shard_map/ppermute | solution.py:732
  382.1 10.7 %collective-permute-done.41 = bf16[144,512]{1,0:T(8,128)(2,1)S(1)} collective-permute-done((bf16[144,512]{1,0:T(8,128)(2,1)S(1)}, bf16[144,512]{1,0:T(8,128)(2,1)S(1)}, u32[]{:S(2)}, u32[]{:S(2)}) %collective-permute-start.41) | collective-permute-done | bytes 147488 | tf_op jit(solution)/shard_map/ppermute | solution.py:732
  408.6 12.3 %collective-permute-done.48 = bf16[144,512]{1,0:T(8,128)(2,1)S(1)} collective-permute-done((bf16[144,512]{1,0:T(8,128)(2,1)S(1)}, bf16[144,512]{1,0:T(8,128)(2,1)S(1)}, u32[]{:S(2)}, u32[]{:S(2)}) %collective-permute-start.48) | collective-permute-done | bytes 147488 | tf_op jit(solution)/shard_map/ppermute | solution.py:732
  420.9 4.4 collective-permute-start.49
  425.4 3.0 multiply_subtract_fusion.1
  431.0 4.8 %qkv_step.1 = (f32[128,2048]{1,0:T(8,128)}, f32[128,2048]{1,0:T(8,128)}, f32[128,2048]{1,0:T(8,128)}, f32[16,512]{1,0:T(8,128)}) custom-call(s32[4]{0:T(128)} %fusion.36.slots, bf16[4,144,512]{2,1,0:T(8,128)(2,1)} %pad_maximum_fusion.4.g_ref, f32[128,2048]{1,0:T(8,128)} %w_ref.2, f32[128,2048]{1,0:T(8,128)} %m_ref.2, f32[128,2048]{1,0:T(8,128)} %v_ref.2), custom_call_target="tpu_custom_call" | custom-call | tf_op jit(solution)/shard_map/qkv_step/pallas_call | solution.py:686
  439.3 6.5 %in_step.1 = (f32[4,2,64,1024]{3,2,1,0:T(8,128)}, f32[4,2,64,1024]{3,2,1,0:T(8,128)}, f32[4,2,64,1024]{3,2,1,0:T(8,128)}) custom-call(bf16[4,64,1024]{2,1,0:T(8,128)(2,1)} %reduce-scatter.6.cloned.1.call-done.gate_ref, bf16[4,64,1024]{2,1,0:T(8,128)(2,1)} %reduce-scatter.8.cloned.1.call-done.up_ref, f32[4,2,64,1024]{3,2,1,0:T(8,128)} %w_ref.3, ...), custom_call_target="tpu_custom_call" | custom-call | tf_op jit(solution)/shard_map/in_step/pallas_call | solution.py:718
  (333 shorter events, 125.6 us)
Async XLA Ops:
  7.2 116.4 %all-gather.8.cloned.1.call-start = ((), (), s32[]{:S(2)}) async-start(), calls=%async_computation.7 | async-start | bytes 2621440 | tf_op jit(solution)/shard_map/all_gather | solution.py:799
  10.0 165.5 %all-gather.10.cloned.1.call-start = ((), (), s32[]{:S(2)}) async-start(), calls=%async_computation.8 | async-start | bytes 2621440 | tf_op jit(solution)/shard_map/all_gather | solution.py:799
  10.8 178.9 %all-gather.6.cloned.1.call-start = ((), (), s32[]{:S(2)}) async-start(), calls=%async_computation.3 | async-start | bytes 2621440 | tf_op jit(solution)/shard_map/all_gather | solution.py:799
  10.8 61.3 %collective-permute-start = (bf16[256,1024]{1,0:T(8,128)(2,1)S(1)}, bf16[256,1024]{1,0:T(8,128)(2,1)}, u32[]{:S(2)}, u32[]{:S(2)}) collective-permute-start(bf16[256,1024]{1,0:T(8,128)(2,1)S(1)} %bitcast.67), channel_id=1, source_target_pairs={{0,16},{16,0},{1,17},{17,1},{2,18},{18,2},{3,19},{19,3},{4,20},{20... | collective-permute-start | bytes 1572872 | tf_op jit(solution)/shard_map/ppermute | solution.py:732
  12.4 66.8 %collective-permute-start.1 = (bf16[256,1024]{1,0:T(8,128)(2,1)S(1)}, bf16[256,1024]{1,0:T(8,128)(2,1)}, u32[]{:S(2)}, u32[]{:S(2)}) collective-permute-start(bf16[256,1024]{1,0:T(8,128)(2,1)S(1)} %bitcast.68), channel_id=1, source_target_pairs={{0,8},{8,0},{1,9},{9,1},{2,10},{10,2},{3,11},{11,3},{4,12},{12,4},... | collective-permute-start | bytes 1572872 | tf_op jit(solution)/shard_map/ppermute | solution.py:732
  16.5 24.6 %collective-permute-start.4 = (bf16[144,512]{1,0:T(8,128)(2,1)}, bf16[144,512]{1,0:T(8,128)(2,1)S(1)}, u32[]{:S(2)}, u32[]{:S(2)}) collective-permute-start(bf16[144,512]{1,0:T(8,128)(2,1)} %get-tuple-element.185), channel_id=1, source_target_pairs={{0,4},{2,6},{4,0},{6,2},{1,5},{3,7},{5,1},{7,3},{8,12},{10,14},{12... | collective-permute-start | bytes 442376 | tf_op jit(solution)/shard_map/ppermute | solution.py:732
  17.8 30.2 %collective-permute-start.5 = (bf16[144,512]{1,0:T(8,128)(2,1)}, bf16[144,512]{1,0:T(8,128)(2,1)}, u32[]{:S(2)}, u32[]{:S(2)}) collective-permute-start(bf16[144,512]{1,0:T(8,128)(2,1)} %get-tuple-element.185), channel_id=1, source_target_pairs={{0,6},{2,0},{4,2},{6,4},{1,7},{3,1},{5,3},{7,5},{8,14},{10,8},{12,... | collective-permute-start | bytes 442376 | tf_op jit(solution)/shard_map/ppermute | solution.py:732
  20.5 286.3 %reduce-scatter.4.cloned.1.call-start = ((), (), s32[]{:S(2)}) async-start(), calls=%async_computation.4 | async-start | bytes 2621440 | tf_op jit(solution)/shard_map/reduce_scatter | solution.py:803
  49.0 16.3 %collective-permute-start.6 = (bf16[4,144,512]{2,1,0:T(8,128)(2,1)S(1)}, bf16[4,144,512]{2,1,0:T(8,128)(2,1)S(1)}, u32[]{:S(2)}, u32[]{:S(2)}) collective-permute-start(bf16[4,144,512]{2,1,0:T(8,128)(2,1)S(1)} %pad_maximum_fusion), channel_id=1, source_target_pairs={{0,1},{1,0},{2,3},{3,2},{4,5},{5,4},{6,7},{7,6},{8,9},{9,8},{10,11... | collective-permute-start | bytes 1769480 | tf_op jit(solution)/shard_map/ppermute | solution.py:732
  50.6 20.4 %collective-permute-start.7 = (bf16[128,1024]{1,0:T(8,128)(2,1)}, bf16[128,1024]{1,0:T(8,128)(2,1)}, u32[]{:S(2)}, u32[]{:S(2)}) collective-permute-start(bf16[128,1024]{1,0:T(8,128)(2,1)} %convert_element_type.294), channel_id=1, source_target_pairs={{0,1},{1,0},{2,3},{3,2},{4,5},{5,4},{6,7},{7,6},{8,9},{9,8},{10,11... | collective-permute-start | bytes 786440 | tf_op jit(solution)/shard_map/ppermute | solution.py:732
  72.2 21.8 %collective-permute-start.10 = (bf16[256,1024]{1,0:T(8,128)(2,1)S(1)}, bf16[256,1024]{1,0:T(8,128)(2,1)}, u32[]{:S(2)}, u32[]{:S(2)}) collective-permute-start(bf16[256,1024]{1,0:T(8,128)(2,1)S(1)} %pad_maximum_fusion.7), channel_id=1, source_target_pairs={{0,6},{10,8},{20,18},{30,28},{1,7},{11,9},{21,19},{31,29}} | collective-permute-start | bytes 1572872 | tf_op jit(solution)/shard_map/ppermute | solution.py:894
  73.7 20.3 %collective-permute-start.9 = (bf16[256,1024]{1,0:T(8,128)(2,1)S(1)}, bf16[256,1024]{1,0:T(8,128)(2,1)}, u32[]{:S(2)}, u32[]{:S(2)}) collective-permute-start(bf16[256,1024]{1,0:T(8,128)(2,1)S(1)} %pad_maximum_fusion.7), channel_id=1, source_target_pairs={{0,4},{10,14},{20,16},{30,26},{1,5},{11,15},{21,17},{31,27}} | collective-permute-start | bytes 1572872 | tf_op jit(solution)/shard_map/ppermute | solution.py:894
  76.2 45.1 %collective-permute-start.8 = (bf16[256,1024]{1,0:T(8,128)(2,1)S(1)}, bf16[256,1024]{1,0:T(8,128)(2,1)}, u32[]{:S(2)}, u32[]{:S(2)}) collective-permute-start(bf16[256,1024]{1,0:T(8,128)(2,1)S(1)} %pad_maximum_fusion.7), channel_id=1, source_target_pairs={{0,2},{10,12},{20,22},{30,24},{1,3},{11,13},{21,23},{31,25}} | collective-permute-start | bytes 1572872 | tf_op jit(solution)/shard_map/ppermute | solution.py:894
  135.8 15.7 %collective-permute-start.16 = (bf16[256,1152]{1,0:T(8,128)(2,1)S(1)}, bf16[256,1152]{1,0:T(8,128)(2,1)S(1)}, u32[]{:S(2)}, u32[]{:S(2)}) collective-permute-start(bf16[256,1152]{1,0:T(8,128)(2,1)S(1)} %pad_maximum_fusion.2), channel_id=1, source_target_pairs={{0,1},{1,0},{2,3},{3,2},{4,5},{5,4},{6,7},{7,6},{8,9},{9,8},{10,11... | collective-permute-start | bytes 1769480 | tf_op jit(solution)/shard_map/ppermute | solution.py:732
  138.1 16.2 %collective-permute-start.17 = (bf16[256,1152]{1,0:T(8,128)(2,1)S(1)}, bf16[256,1152]{1,0:T(8,128)(2,1)S(1)}, u32[]{:S(2)}, u32[]{:S(2)}) collective-permute-start(bf16[256,1152]{1,0:T(8,128)(2,1)S(1)} %pad_maximum_fusion.3), channel_id=1, source_target_pairs={{0,16},{16,0},{1,17},{17,1},{2,18},{18,2},{3,19},{19,3},{4,20},{20... | collective-permute-start | bytes 1769480 | tf_op jit(solution)/shard_map/ppermute | solution.py:732
  138.3 26.5 %collective-permute-start.13 = (bf16[256,1024]{1,0:T(8,128)(2,1)S(1)}, bf16[256,1024]{1,0:T(8,128)(2,1)S(1)}, u32[]{:S(2)}, u32[]{:S(2)}) collective-permute-start(bf16[256,1024]{1,0:T(8,128)(2,1)S(1)} %add_convert_fusion.14), channel_id=1, source_target_pairs={{0,16},{16,0},{1,17},{17,1},{2,18},{18,2},{3,19},{19,3},{4,20},{20... | collective-permute-start | bytes 1572872 | tf_op jit(solution)/shard_map/ppermute | solution.py:732
  225.1 179.8 %reduce-scatter.6.cloned.1.call-start = ((), (), s32[]{:S(2)}) async-start(), calls=%async_computation.5 | async-start | bytes 2621440 | tf_op jit(solution)/shard_map/reduce_scatter | solution.py:803
  253.5 14.3 %collective-permute-start.30 = (bf16[256,1024]{1,0:T(8,128)(2,1)}, bf16[256,1024]{1,0:T(8,128)(2,1)}, u32[]{:S(2)}, u32[]{:S(2)}) collective-permute-start(bf16[256,1024]{1,0:T(8,128)(2,1)} %slice.156), channel_id=1, source_target_pairs={{0,16},{16,0},{1,17},{17,1},{2,18},{18,2},{3,19},{19,3},{4,20},{20... | collective-permute-start | bytes 1572872 | tf_op jit(solution)/shard_map/ppermute | solution.py:732
  256.5 14.3 %collective-permute-start.27 = (bf16[256,1024]{1,0:T(8,128)(2,1)}, bf16[256,1024]{1,0:T(8,128)(2,1)}, u32[]{:S(2)}, u32[]{:S(2)}) collective-permute-start(bf16[256,1024]{1,0:T(8,128)(2,1)} %slice.152), channel_id=1, source_target_pairs={{0,1},{1,0},{2,3},{3,2},{4,5},{5,4},{6,7},{7,6},{8,9},{9,8},{10,11... | collective-permute-start | bytes 1572872 | tf_op jit(solution)/shard_map/ppermute | solution.py:732
  274.2 165.2 %reduce-scatter.8.cloned.1.call-start = ((), (), s32[]{:S(2)}) async-start(), calls=%async_computation.6 | async-start | bytes 2621440 | tf_op jit(solution)/shard_map/reduce_scatter | solution.py:803
  331.2 21.7 %collective-permute-start.38 = (bf16[4,144,512]{2,1,0:T(8,128)(2,1)}, bf16[4,144,512]{2,1,0:T(8,128)(2,1)}, u32[]{:S(2)}, u32[]{:S(2)}) collective-permute-start(bf16[4,144,512]{2,1,0:T(8,128)(2,1)} %get-tuple-element.143), channel_id=1, source_target_pairs={{0,1},{1,0},{2,3},{3,2},{4,5},{5,4},{6,7},{7,6},{8,9},{9,8},{10,11... | collective-permute-start | bytes 1769480 | tf_op jit(solution)/shard_map/ppermute | solution.py:732
  334.7 59.4 %collective-permute-start.45 = (bf16[256,1024]{1,0:T(8,128)(2,1)S(1)}, bf16[256,1024]{1,0:T(8,128)(2,1)S(1)}, u32[]{:S(2)}, u32[]{:S(2)}) collective-permute-start(bf16[256,1024]{1,0:T(8,128)(2,1)S(1)} %slice.164), channel_id=1, source_target_pairs={{0,16},{16,0},{1,17},{17,1},{2,18},{18,2},{3,19},{19,3},{4,20},{20... | collective-permute-start | bytes 1572872 | tf_op jit(solution)/shard_map/ppermute | solution.py:732
  340.2 56.5 %collective-permute-start.34 = (bf16[256,1024]{1,0:T(8,128)(2,1)S(1)}, bf16[256,1024]{1,0:T(8,128)(2,1)S(1)}, u32[]{:S(2)}, u32[]{:S(2)}) collective-permute-start(bf16[256,1024]{1,0:T(8,128)(2,1)S(1)} %slice.160), channel_id=1, source_target_pairs={{0,1},{1,0},{2,3},{3,2},{4,5},{5,4},{6,7},{7,6},{8,9},{9,8},{10,11... | collective-permute-start | bytes 1572872 | tf_op jit(solution)/shard_map/ppermute | solution.py:732
  355.6 25.8 %collective-permute-start.42 = (bf16[144,512]{1,0:T(8,128)(2,1)S(1)}, bf16[144,512]{1,0:T(8,128)(2,1)S(1)}, u32[]{:S(2)}, u32[]{:S(2)}) collective-permute-start(bf16[144,512]{1,0:T(8,128)(2,1)S(1)} %get-tuple-element.194), channel_id=1, source_target_pairs={{0,4},{2,6},{4,0},{6,2},{1,5},{3,7},{5,1},{7,3},{8,12},{10,14},{12... | collective-permute-start | bytes 442376 | tf_op jit(solution)/shard_map/ppermute | solution.py:732
  360.1 32.6 %collective-permute-start.41 = (bf16[144,512]{1,0:T(8,128)(2,1)S(1)}, bf16[144,512]{1,0:T(8,128)(2,1)S(1)}, u32[]{:S(2)}, u32[]{:S(2)}) collective-permute-start(bf16[144,512]{1,0:T(8,128)(2,1)S(1)} %get-tuple-element.192), channel_id=1, source_target_pairs={{0,6},{2,0},{4,2},{6,4},{1,7},{3,1},{5,3},{7,5},{8,14},{10,8},{12,... | collective-permute-start | bytes 442376 | tf_op jit(solution)/shard_map/ppermute | solution.py:732
  368.1 29.6 %collective-permute-start.54 = (bf16[128,1024]{1,0:T(8,128)(2,1)S(1)}, bf16[128,1024]{1,0:T(8,128)(2,1)S(1)}, u32[]{:S(2)}, u32[]{:S(2)}) collective-permute-start(bf16[128,1024]{1,0:T(8,128)(2,1)S(1)} %add_convert_fusion.17), channel_id=1, source_target_pairs={{6,0},{8,10},{18,20},{28,30},{7,1},{9,11},{19,21},{29,31}} | collective-permute-start | bytes 786440 | tf_op jit(solution)/shard_map/ppermute | solution.py:986
  381.4 16.3 %collective-permute-start.53 = (bf16[128,1024]{1,0:T(8,128)(2,1)S(1)}, bf16[128,1024]{1,0:T(8,128)(2,1)S(1)}, u32[]{:S(2)}, u32[]{:S(2)}) collective-permute-start(bf16[128,1024]{1,0:T(8,128)(2,1)S(1)} %add_convert_fusion.17), channel_id=1, source_target_pairs={{4,0},{14,10},{16,20},{26,30},{5,1},{15,11},{17,21},{27,31}} | collective-permute-start | bytes 786440 | tf_op jit(solution)/shard_map/ppermute | solution.py:986
  400.2 25.1 %collective-permute-start.57 = (bf16[128,1024]{1,0:T(8,128)(2,1)}, bf16[128,1024]{1,0:T(8,128)(2,1)}, u32[]{:S(2)}, u32[]{:S(2)}) collective-permute-start(bf16[128,1024]{1,0:T(8,128)(2,1)} %add_convert_fusion.16), channel_id=1, source_target_pairs={{0,24},{10,2},{20,12},{30,22},{1,25},{11,3},{21,13},{31,23}} | collective-permute-start | bytes 786440 | tf_op jit(solution)/shard_map/ppermute | solution.py:998
  401.5 23.8 %collective-permute-start.56 = (bf16[128,1024]{1,0:T(8,128)(2,1)}, bf16[128,1024]{1,0:T(8,128)(2,1)}, u32[]{:S(2)}, u32[]{:S(2)}) collective-permute-start(bf16[128,1024]{1,0:T(8,128)(2,1)} %add_convert_fusion.16), channel_id=1, source_target_pairs={{0,16},{10,26},{20,4},{30,14},{1,17},{11,27},{21,5},{31,15}} | collective-permute-start | bytes 786440 | tf_op jit(solution)/shard_map/ppermute | solution.py:998
  402.9 22.5 %collective-permute-start.55 = (bf16[128,1024]{1,0:T(8,128)(2,1)}, bf16[128,1024]{1,0:T(8,128)(2,1)}, u32[]{:S(2)}, u32[]{:S(2)}) collective-permute-start(bf16[128,1024]{1,0:T(8,128)(2,1)} %add_convert_fusion.16), channel_id=1, source_target_pairs={{0,8},{10,18},{20,28},{30,6},{1,9},{11,19},{21,29},{31,7}} | collective-permute-start | bytes 786440 | tf_op jit(solution)/shard_map/ppermute | solution.py:998
  404.9 33.6 %collective-permute-start.47 = (bf16[256,1024]{1,0:T(8,128)(2,1)}, bf16[256,1024]{1,0:T(8,128)(2,1)S(1)}, u32[]{:S(2)}, u32[]{:S(2)}) collective-permute-start(bf16[256,1024]{1,0:T(8,128)(2,1)} %add_convert_fusion.9), channel_id=1, source_target_pairs={{0,16},{16,0},{1,17},{17,1},{2,18},{18,2},{3,19},{19,3},{4,20},{20... | collective-permute-start | bytes 1572872 | tf_op jit(solution)/shard_map/ppermute | solution.py:732
  405.2 15.7 %collective-permute-start.48 = (bf16[144,512]{1,0:T(8,128)(2,1)S(1)}, bf16[144,512]{1,0:T(8,128)(2,1)S(1)}, u32[]{:S(2)}, u32[]{:S(2)}) collective-permute-start(bf16[144,512]{1,0:T(8,128)(2,1)S(1)} %fusion.25), channel_id=1, source_target_pairs={{0,16},{16,0},{1,17},{17,1},{2,18},{18,2},{3,19},{19,3},{4,20},{20... | collective-permute-start | bytes 442376 | tf_op jit(solution)/shard_map/ppermute | solution.py:732
  (98 other events, 1143.6 us)
Sparse Core Ops, SparseCore 0:
  10.2 53.8 all-gather.7
  66.3 60.9 all-gather.9
  128.8 48.1 all-gather.5
  225.2 42.5 reduce-scatter.3
  274.3 42.4 reduce-scatter.5
  333.6 62.3 reduce-scatter.7

commit v2 on v1

--- a/solution.py
+++ b/solution.py
@@ -887,8 +887,8 @@
     x_all = collect_expert(tokens[0])
     cosine, sine = rotary_tables(length)
 
-    out_pair = jnp.concatenate(collect(after(out_w.astype(low), w_deep), "y"), axis=0)
-    out_pair = after(out_pair, w_all)
+    out_pair = jnp.concatenate(collect(out_w.astype(low), "y"), axis=0)
+    out_pair = after(out_pair, w_deep)
     out_all = jnp.where(at_z == own, out_pair, jnp.zeros_like(out_pair))
     for moves in diagonal_moves(False):
         out_all = out_all + lax.ppermute(out_pair, joint, moves)
@@ -953,7 +953,8 @@
     down_new = adam_step(
         expert_out, down_m, down_v, down_total.astype(high), 3.0 * (FF // 16) ** (-0.5), weight_decay
     )
-    grad_all[0] = after(grad_all[0], out_units[0], *mixed, down_new[0])
+    out_piece = give_back(out_units, "y")
+    grad_all[0] = after(grad_all[0], out_piece, *mixed, down_new[0])
     qkv_grad, norm_one_grad = attend_back(
         blocks,
         shard_at,
@@ -974,28 +975,27 @@
         gain_two_grad,
     )
     qkv_sum = give_back(qkv_grad, "y")
-    out_piece = give_back(out_units, "y", qkv_grad)
     norm_one_core = give_back_core(norm_one_grad)
     qkv_total = give_back(after(qkv_sum, *norm_one_core), DEEP)
     upper = give_back_rows(mixed[0], "y", (qkv_total,))
     lower = give_back_rows(mixed[1], "x", (qkv_total,))
     norm_one_low = give_back(norm_one_core, "x", (qkv_total,))
+    qkv_total, gate_total = lax.optimization_barrier((qkv_total, gate_total))
+    qkv_pieces = collect_expert(qkv_total)
     scale_one = rms_scale(inputs)
     out_total = out_piece.astype(high)
     for moves in diagonal_moves(False):
         moved = lax.ppermute(out_piece, joint, [(b, a) for a, b in moves])
-        out_total = out_total + after(moved, qkv_total).astype(high)
+        out_total = out_total + after(moved, qkv_sum).astype(high)
     out_piece = out_total.astype(low)
     norm_one_grad = norm_one_low.astype(high)
     input_grad = middle_grad + norm_back(inputs, scale_one, gain_one, norm_one_grad)
     mixed = give_back_second(upper, lower)
     output = (middle + mixed.astype(high)).astype(low)
-    qkv_total, gate_total = lax.optimization_barrier((qkv_total, gate_total))
-    qkv_pieces = collect_expert(qkv_total)
     qkv_total = jnp.stack(qkv_pieces)
     out_total = jnp.where(at_z == own, out_piece, jnp.zeros_like(out_piece))
     for moves in diagonal_moves(True):
-        out_total = out_total + lax.ppermute(out_piece, joint, moves)
+        out_total = out_total + after(lax.ppermute(out_piece, joint, moves), *qkv_pieces[1:])
     gate_total, up_total = lax.optimization_barrier((gate_total, up_total, *qkv_pieces[1:]))[:2]
 
     rate = 3.0 * D ** (-0.5)

time: 463 us -> 437 us (0.944)
  waiting for transfers between devices: 179 us -> 132 us
  starting transfers between devices: 60.1 us -> 86.2 us
    ppermute x49, waiting for transfers between devices: 150 us -> 104 us  [shifted(): lax.ppermute(value, axis, [(j, (j + step) % size) for j in range(size)])]
    ppermute x49, starting transfers between devices: 48.8 us -> 70.8 us  [shifted(): lax.ppermute(value, axis, [(j, (j + step) % size) for j in range(size)])]
    ppermute x3, waiting for transfers between devices: 27.4 us -> 10.2 us  [body(): out_all = out_all + lax.ppermute(out_pair, joint, moves)]
    all_gather x3, waiting for transfers between devices: 0.01 us -> 8.42 us  [collect_weight(): return lax.all_gather(shard.astype(low), DEEP, axis=1, tiled=True)]
    ppermute x3, waiting for transfers between devices: 1.69 us -> 8.35 us  [body(): moved = lax.ppermute(out_piece, joint, [(b, a) for a, b in moves])]
    unnamed x139 -> x133, local copies, waits for them, and re-layouts: 9.49 us -> 10.5 us
  transfers between devices with their start and end apart: 64 -> 64, of which waited for: 27 -> 25; matrix products, arithmetic and copies ran while one was open for 14% -> 14% of each run, Pallas kernels for 19% -> 20%
where the time goes in v2:
time: 437 us; the launch traced here: 429 us
  waiting for transfers between devices  132 us (30%)
  Pallas kernels  127 us (29%)
  starting transfers between devices  86.2 us (20%)
  other arithmetic  47.2 us (11%)
  local copies, waits for them, and re-layouts  21.9 us (5%)
  between operations  15.5 us (4%)
    ppermute x49, waiting for transfers between devices, shifted(): lax.ppermute(value, axis, [(j, (j + step) % size) for j in range(size)])  104 us
    ppermute x49, starting transfers between devices, shifted(): lax.ppermute(value, axis, [(j, (j + step) % size) for j in range(size)])  70.8 us
    pallas_call x1, Pallas kernels, run_experts(): pl.pallas_call(experts_kernel, grid=(len(h_all),), out_shape=(jax.ShapeDt...  32.4 us
    pallas_call x1, Pallas kernels, attend_back(): pl.pallas_call(functools.partial(attend_back_kernel, count, heads, keys,...  19.5 us
    pallas_call x2, Pallas kernels, weight_grads(): pl.pallas_call(weight_grads_kernel, grid=(owned,), out_shape=(jax.ShapeDt...  17.4 us
    pallas_call x1, Pallas kernels, back_rows(): pl.pallas_call(back_rows_kernel, grid=(4,), out_shape=(jax.ShapeDtypeStru...  16.6 us
    convert_element_type x19, other arithmetic, give_back(): return total.astype(low)  14.5 us
    pallas_call x1, Pallas kernels, attend(): pl.pallas_call(functools.partial(attend_kernel, count, heads, keys), out_...  13.9 us
  transfers between devices with their start and end apart: 64, of which 25 were waited for; matrix products, arithmetic and copies ran while one was open for 14% of the time, Pallas kernels for 20%

profile of v2, /device:TPU:8, one launch (start us, length us, event | category | flops | bytes accessed | tf_op | source)
XLA Modules:
  0.0 429.2 jit_solution(1546977989813974427)
XLA Ops:
  28.6 10.4 %collective-permute-done.4 = bf16[144,512]{1,0:T(8,128)(2,1)} collective-permute-done((bf16[144,512]{1,0:T(8,128)(2,1)}, bf16[144,512]{1,0:T(8,128)(2,1)}, u32[]{:S(2)}, u32[]{:S(2)}) %collective-permute-start.4) | collective-permute-done | bytes 147488 | tf_op jit(solution)/shard_map/ppermute | solution.py:732
  39.0 6.8 %collective-permute-done.5 = bf16[144,512]{1,0:T(8,128)(2,1)} collective-permute-done((bf16[144,512]{1,0:T(8,128)(2,1)}, bf16[144,512]{1,0:T(8,128)(2,1)}, u32[]{:S(2)}, u32[]{:S(2)}) %collective-permute-start.5) | collective-permute-done | bytes 147488 | tf_op jit(solution)/shard_map/ppermute | solution.py:732
  56.5 5.5 %collective-permute-done.6 = bf16[4,144,512]{2,1,0:T(8,128)(2,1)S(1)} collective-permute-done((bf16[4,144,512]{2,1,0:T(8,128)(2,1)S(1)}, bf16[4,144,512]{2,1,0:T(8,128)(2,1)S(1)}, u32[]{:S(2)}, u32[]{:S(2)}) %collective-permute-start.6) | collective-permute-done | bytes 589856 | tf_op jit(solution)/shard_map/ppermute | solution.py:732
  66.3 10.2 %collective-permute-done.8 = bf16[256,1024]{1,0:T(8,128)(2,1)} collective-permute-done((bf16[256,1024]{1,0:T(8,128)(2,1)S(1)}, bf16[256,1024]{1,0:T(8,128)(2,1)}, u32[]{:S(2)}, u32[]{:S(2)}) %collective-permute-start.8) | collective-permute-done | bytes 524320 | tf_op jit(solution)/shard_map/ppermute | solution.py:894
  80.9 13.9 %attend.1 = (bf16[1024,1024]{1,0:T(8,128)(2,1)}, bf16[1024,512]{1,0:T(8,128)(2,1)}, bf16[32,1024]{1,0:T(8,128)(2,1)}, bf16[4,1024,64]{2,1,0:T(8,128)(2,1)}, bf16...) custom-call(s32[4]{0:T(128)} %fusion.33.blocks, ...), custom_call_target="tpu_custom_call" | custom-call | tf_op jit(solution)/shard_map/attend/pallas_call | solution.py:171
  97.6 7.9 %collective-permute-start.12 = (bf16[256,1024]{1,0:T(8,128)(2,1)}, bf16[256,1024]{1,0:T(8,128)(2,1)S(1)}, u32[]{:S(2)}, u32[]{:S(2)}) collective-permute-start(bf16[256,1024]{1,0:T(8,128)(2,1)} %get-tuple-element.101), channel_id=1, source_target_pairs={{0,8},{8,0},{1,9},{9,1},{2,10},{10,2},{3,11},{11,3},{4,12},{12,4},... | collective-permute-start | bytes 1572872 | tf_op jit(solution)/shard_map/ppermute | solution.py:732
  109.3 3.8 collective-permute-start.17
  114.3 8.2 %collective-permute-done.16 = bf16[256,1152]{1,0:T(8,128)(2,1)S(1)} collective-permute-done((bf16[256,1152]{1,0:T(8,128)(2,1)S(1)}, bf16[256,1152]{1,0:T(8,128)(2,1)S(1)}, u32[]{:S(2)}, u32[]{:S(2)}) %collective-permute-start.16) | collective-permute-done | bytes 589856 | tf_op jit(solution)/shard_map/ppermute | solution.py:732
  123.4 3.8 collective-permute-done.17
  128.1 9.5 %collective-permute-done.13 = bf16[256,1024]{1,0:T(8,128)(2,1)S(1)} collective-permute-done((bf16[256,1024]{1,0:T(8,128)(2,1)S(1)}, bf16[256,1024]{1,0:T(8,128)(2,1)S(1)}, u32[]{:S(2)}, u32[]{:S(2)}) %collective-permute-start.13) | collective-permute-done | bytes 524320 | tf_op jit(solution)/shard_map/ppermute | solution.py:732
  140.8 5.3 %collective-permute-done.18 = bf16[128,1024]{1,0:T(8,128)(2,1)S(1)} collective-permute-done((bf16[128,1024]{1,0:T(8,128)(2,1)S(1)}, bf16[128,1024]{1,0:T(8,128)(2,1)S(1)}, u32[]{:S(2)}, u32[]{:S(2)}) %collective-permute-start.18) | collective-permute-done | bytes 262176 | tf_op jit(solution)/shard_map/ppermute | solution.py:732
  152.3 8.0 %collective-permute-done.20 = bf16[256,1024]{1,0:T(8,128)(2,1)S(1)} collective-permute-done((bf16[256,1024]{1,0:T(8,128)(2,1)}, bf16[256,1024]{1,0:T(8,128)(2,1)S(1)}, u32[]{:S(2)}, u32[]{:S(2)}) %collective-permute-start.20) | collective-permute-done | bytes 524320 | tf_op jit(solution)/shard_map/ppermute | solution.py:732
  161.7 8.4 %all-gather.6.cloned.1.call-done.down_ref = bf16[4,256,1024]{2,1,0:T(8,128)(2,1)} async-done(((bf16[4,64,1024]{2,1,0:T(8,128)(2,1)}), bf16[4,256,1024]{2,1,0:T(8,128)(2,1)}) %all-gather.6.cloned.1.call-update) | async-done | bytes 2097168 | tf_op jit(solution)/shard_map/all_gather | solution.py:799
  170.2 32.4 %experts.1 = (bf16[2048,1024]{1,0:T(8,128)(2,1)}, bf16[2048,1024]{1,0:T(8,128)(2,1)}, bf16[2048,1024]{1,0:T(8,128)(2,1)}, bf16[2048,16]{1,0:T(8,128)(2,1)}, f32[...) custom-call(s32[1]{0:T(128)} %bitcast.10.first, bf16[512,1024]{1,0:T(8,128)(2,1)} %copy-done.4, ...), custom_call_target="tpu_custom_call" | custom-call | tf_op jit(solution)/shard_map/experts/pallas_call | solution.py:315
  202.7 16.6 %back_rows.1 = (bf16[512,1024]{1,0:T(8,128)(2,1)}, bf16[512,1024]{1,0:T(8,128)(2,1)}, bf16[512,1024]{1,0:T(8,128)(2,1)}, bf16[512,1024]{1,0:T(8,128)(2,1)}) custom-call(bf16[2048,1024]{1,0:T(8,128)(2,1)} %get-tuple-element.117.gate_grad_ref.grad_ref, bf16[2048,1024]{1,0:T(8,128)(2,1)} %get-tuple-element.120.up_grad_ref.grad_ref, ...), custom_call_target="tpu_custom_call" | custom-call | tf_op jit(solution)/shard_map/back_rows/pallas_call | solution.py:371
  219.8 8.7 %weight_grads.2 = bf16[4,256,1024]{2,1,0:T(8,128)(2,1)} custom-call(bf16[2048,1024]{1,0:T(8,128)(2,1)} %get-tuple-element.117.gate_grad_ref.grad_ref, bf16[512,1024]{1,0:T(8,128)(2,1)} %copy-done.4, bf16[512,1024]{1,0:T(8,128)(2,1)} %copy-done.3, bf16[512,1024]{1,0:T(8,128)(2,1)} %collective-permute-done.22.h_2, bf16[512,1024]{1,0:T(8,128)(2,1)} %collective-permute-done.23.h_3), custom_call_target="tpu_custom_call" | custom-call | tf_op jit(solution)/shard_map/weight_grads/pallas_call | solution.py:407
  236.5 8.7 %weight_grads.3 = bf16[4,256,1024]{2,1,0:T(8,128)(2,1)} custom-call(bf16[2048,1024]{1,0:T(8,128)(2,1)} %get-tuple-element.120.up_grad_ref.grad_ref, bf16[512,1024]{1,0:T(8,128)(2,1)} %copy-done.4, bf16[512,1024]{1,0:T(8,128)(2,1)} %copy-done.3, bf16[512,1024]{1,0:T(8,128)(2,1)} %collective-permute-done.22.h_2, bf16[512,1024]{1,0:T(8,128)(2,1)} %collective-permute-done.23.h_3), custom_call_target="tpu_custom_call" | custom-call | tf_op jit(solution)/shard_map/weight_grads/pallas_call | solution.py:407
  254.3 3.5 collective-permute-done.29
  260.9 9.6 %expert_results.1 = (bf16[512,1024]{1,0:T(8,128)(2,1)}, bf16[512,1024]{1,0:T(8,128)(2,1)}, bf16[512,1024]{1,0:T(8,128)(2,1)}, bf16[512,1024]{1,0:T(8,128)(2,1)}) custom-call(bf16[2048,1024]{1,0:T(8,128)(2,1)} %get-tuple-element.123.act_ref, bf16[1024,1024]{1,0:T(8,128)(2,1)} %bitcast.69), custom_call_target="tpu_custom_call" | custom-call | tf_op jit(solution)/shard_map/expert_results/pallas_call | solution.py:432
  272.3 3.1 collective-permute-done.35.refs_2_
  277.7 3.3 out_grads.1
  283.0 6.5 %collective-permute-done.37 = bf16[128,1024]{1,0:T(8,128)(2,1)S(1)} collective-permute-done((bf16[128,1024]{1,0:T(8,128)(2,1)}, bf16[128,1024]{1,0:T(8,128)(2,1)S(1)}, u32[]{:S(2)}, u32[]{:S(2)}) %collective-permute-start.37) | collective-permute-done | bytes 262176 | tf_op jit(solution)/shard_map/ppermute | solution.py:732
  293.3 4.3 %multiply_subtract_fusion = (f32[4,64,1024]{2,1,0:T(8,128)}, f32[4,64,1024]{2,1,0:T(8,128)}, f32[4,64,1024]{2,1,0:T(8,128)}) fusion(f32[4,64,1024]{2,1,0:T(8,128)} %param.39, bf16[4,64,1024]{2,1,0:T(8,128)(2,1)} %reduce-scatter.4.cloned.1.call-done, f32[4,64,1024]{2,1,0:T(8,128)} %param.41, f32[4,64,1024]{2,1,0:T(8,128)} %param.40), kind=kLoop, calls=%fused_computation.29 | loop fusion | flops 4194304 | bytes 6815744 | tf_op jit(solution)/shard_map/sub | solution.py:68
  297.6 19.5 %attend_back.1 = (bf16[4,144,512]{2,1,0:T(8,128)(2,1)}, bf16[4,144,512]{2,1,0:T(8,128)(2,1)}, bf16[256,1024]{1,0:T(8,128)(2,1)}, bf16[256,1024]{1,0:T(8,128)(2,1...) custom-call(s32[4]{0:T(128)} %fusion.33.blocks, s32[8]{0:T(128)} %fusion.35.shard_at, ...), custom_call_target="tpu_custom_call" | custom-call | tf_op jit(solution)/shard_map/attend_back/pallas_call | solution.py:608
  322.2 5.5 %collective-permute-start.52 = (bf16[128,1024]{1,0:T(8,128)(2,1)S(1)}, bf16[128,1024]{1,0:T(8,128)(2,1)S(1)}, u32[]{:S(2)}, u32[]{:S(2)}) collective-permute-start(bf16[128,1024]{1,0:T(8,128)(2,1)S(1)} %add_convert_fusion.19), channel_id=1, source_target_pairs={{2,0},{12,10},{22,20},{24,30},{3,1},{13,11},{23,21},{25,31}} | collective-permute-start | bytes 786440 | tf_op jit(solution)/shard_map/ppermute | solution.py:988
  337.0 4.5 %collective-permute-start.43 = (bf16[144,512]{1,0:T(8,128)(2,1)S(1)}, bf16[144,512]{1,0:T(8,128)(2,1)S(1)}, u32[]{:S(2)}, u32[]{:S(2)}) collective-permute-start(bf16[144,512]{1,0:T(8,128)(2,1)S(1)} %get-tuple-element.196), channel_id=1, source_target_pairs={{0,4},{2,6},{4,0},{6,2},{1,5},{3,7},{5,1},{7,3},{8,12},{10,14},{12... | collective-permute-start | bytes 442376 | tf_op jit(solution)/shard_map/ppermute | solution.py:732
  341.5 8.3 %collective-permute-done.52 = bf16[128,1024]{1,0:T(8,128)(2,1)S(1)} collective-permute-done((bf16[128,1024]{1,0:T(8,128)(2,1)S(1)}, bf16[128,1024]{1,0:T(8,128)(2,1)S(1)}, u32[]{:S(2)}, u32[]{:S(2)}) %collective-permute-start.52) | collective-permute-done | bytes 262176 | tf_op jit(solution)/shard_map/ppermute | solution.py:988
  349.8 12.2 %collective-permute-start.42 = (bf16[144,512]{1,0:T(8,128)(2,1)S(1)}, bf16[144,512]{1,0:T(8,128)(2,1)S(1)}, u32[]{:S(2)}, u32[]{:S(2)}) collective-permute-start(bf16[144,512]{1,0:T(8,128)(2,1)S(1)} %get-tuple-element.194), channel_id=1, source_target_pairs={{0,6},{2,0},{4,2},{6,4},{1,7},{3,1},{5,3},{7,5},{8,14},{10,8},{12,... | collective-permute-start | bytes 442376 | tf_op jit(solution)/shard_map/ppermute | solution.py:732
  362.7 17.9 %collective-permute-done.42 = bf16[144,512]{1,0:T(8,128)(2,1)S(1)} collective-permute-done((bf16[144,512]{1,0:T(8,128)(2,1)S(1)}, bf16[144,512]{1,0:T(8,128)(2,1)S(1)}, u32[]{:S(2)}, u32[]{:S(2)}) %collective-permute-start.42) | collective-permute-done | bytes 147488 | tf_op jit(solution)/shard_map/ppermute | solution.py:732
  394.0 3.5 collective-permute-start.50
  401.4 4.8 %qkv_step.1 = (f32[128,2048]{1,0:T(8,128)}, f32[128,2048]{1,0:T(8,128)}, f32[128,2048]{1,0:T(8,128)}, f32[16,512]{1,0:T(8,128)}) custom-call(s32[4]{0:T(128)} %fusion.36.slots, bf16[4,144,512]{2,1,0:T(8,128)(2,1)} %pad_maximum_fusion.4.g_ref, f32[128,2048]{1,0:T(8,128)} %w_ref.2, f32[128,2048]{1,0:T(8,128)} %m_ref.2, f32[128,2048]{1,0:T(8,128)} %v_ref.2), custom_call_target="tpu_custom_call" | custom-call | tf_op jit(solution)/shard_map/qkv_step/pallas_call | solution.py:686
  413.6 6.6 %in_step.1 = (f32[4,2,64,1024]{3,2,1,0:T(8,128)}, f32[4,2,64,1024]{3,2,1,0:T(8,128)}, f32[4,2,64,1024]{3,2,1,0:T(8,128)}) custom-call(bf16[4,64,1024]{2,1,0:T(8,128)(2,1)} %reduce-scatter.6.cloned.1.call-done.gate_ref, bf16[4,64,1024]{2,1,0:T(8,128)(2,1)} %reduce-scatter.8.cloned.1.call-done.up_ref, f32[4,2,64,1024]{3,2,1,0:T(8,128)} %w_ref.3, ...), custom_call_target="tpu_custom_call" | custom-call | tf_op jit(solution)/shard_map/in_step/pallas_call | solution.py:718
  (327 shorter events, 132.2 us)
Async XLA Ops:
  7.2 87.6 %all-gather.8.cloned.1.call-start = ((), (), s32[]{:S(2)}) async-start(), calls=%async_computation.7 | async-start | bytes 2621440 | tf_op jit(solution)/shard_map/all_gather | solution.py:799
  10.0 138.0 %all-gather.10.cloned.1.call-start = ((), (), s32[]{:S(2)}) async-start(), calls=%async_computation.8 | async-start | bytes 2621440 | tf_op jit(solution)/shard_map/all_gather | solution.py:799
  10.7 159.4 %all-gather.6.cloned.1.call-start = ((), (), s32[]{:S(2)}) async-start(), calls=%async_computation.3 | async-start | bytes 2621440 | tf_op jit(solution)/shard_map/all_gather | solution.py:799
  14.9 24.0 %collective-permute-start.4 = (bf16[144,512]{1,0:T(8,128)(2,1)}, bf16[144,512]{1,0:T(8,128)(2,1)}, u32[]{:S(2)}, u32[]{:S(2)}) collective-permute-start(bf16[144,512]{1,0:T(8,128)(2,1)} %get-tuple-element.187), channel_id=1, source_target_pairs={{0,4},{2,6},{4,0},{6,2},{1,5},{3,7},{5,1},{7,3},{8,12},{10,14},{12... | collective-permute-start | bytes 442376 | tf_op jit(solution)/shard_map/ppermute | solution.py:732
  16.0 29.8 %collective-permute-start.5 = (bf16[144,512]{1,0:T(8,128)(2,1)}, bf16[144,512]{1,0:T(8,128)(2,1)}, u32[]{:S(2)}, u32[]{:S(2)}) collective-permute-start(bf16[144,512]{1,0:T(8,128)(2,1)} %get-tuple-element.187), channel_id=1, source_target_pairs={{0,6},{2,0},{4,2},{6,4},{1,7},{3,1},{5,3},{7,5},{8,14},{10,8},{12,... | collective-permute-start | bytes 442376 | tf_op jit(solution)/shard_map/ppermute | solution.py:732
  18.0 46.3 %collective-permute-start = (bf16[256,1024]{1,0:T(8,128)(2,1)S(1)}, bf16[256,1024]{1,0:T(8,128)(2,1)}, u32[]{:S(2)}, u32[]{:S(2)}) collective-permute-start(bf16[256,1024]{1,0:T(8,128)(2,1)S(1)} %bitcast.67), channel_id=1, source_target_pairs={{0,16},{16,0},{1,17},{17,1},{2,18},{18,2},{3,19},{19,3},{4,20},{20... | collective-permute-start | bytes 1572872 | tf_op jit(solution)/shard_map/ppermute | solution.py:732
  19.5 31.8 %collective-permute-start.7 = (bf16[128,1024]{1,0:T(8,128)(2,1)S(1)}, bf16[128,1024]{1,0:T(8,128)(2,1)}, u32[]{:S(2)}, u32[]{:S(2)}) collective-permute-start(bf16[128,1024]{1,0:T(8,128)(2,1)S(1)} %convert_element_type.294), channel_id=1, source_target_pairs={{0,1},{1,0},{2,3},{3,2},{4,5},{5,4},{6,7},{7,6},{8,9},{9,8},{10,11... | collective-permute-start | bytes 786440 | tf_op jit(solution)/shard_map/ppermute | solution.py:732
  22.0 271.3 %reduce-scatter.4.cloned.1.call-start = ((), (), s32[]{:S(2)}) async-start(), calls=%async_computation.4 | async-start | bytes 2621440 | tf_op jit(solution)/shard_map/reduce_scatter | solution.py:803
  55.2 21.3 %collective-permute-start.8 = (bf16[256,1024]{1,0:T(8,128)(2,1)S(1)}, bf16[256,1024]{1,0:T(8,128)(2,1)}, u32[]{:S(2)}, u32[]{:S(2)}) collective-permute-start(bf16[256,1024]{1,0:T(8,128)(2,1)S(1)} %pad_maximum_fusion.7), channel_id=1, source_target_pairs={{0,2},{10,12},{20,22},{30,24},{1,3},{11,13},{21,23},{31,25}} | collective-permute-start | bytes 1572872 | tf_op jit(solution)/shard_map/ppermute | solution.py:894
  62.2 16.6 %collective-permute-start.14 = (bf16[128,1152]{1,0:T(8,128)(2,1)S(1)}, bf16[128,1152]{1,0:T(8,128)(2,1)}, u32[]{:S(2)}, u32[]{:S(2)}) collective-permute-start(bf16[128,1152]{1,0:T(8,128)(2,1)S(1)} %get-tuple-element.198), channel_id=1, source_target_pairs={{0,16},{16,0},{1,17},{17,1},{2,18},{18,2},{3,19},{19,3},{4,20},{20... | collective-permute-start | bytes 884744 | tf_op jit(solution)/shard_map/ppermute | solution.py:732
  64.3 15.6 %collective-permute-start.1 = (bf16[256,1024]{1,0:T(8,128)(2,1)S(1)}, bf16[256,1024]{1,0:T(8,128)(2,1)S(1)}, u32[]{:S(2)}, u32[]{:S(2)}) collective-permute-start(bf16[256,1024]{1,0:T(8,128)(2,1)S(1)} %bitcast.68), channel_id=1, source_target_pairs={{0,8},{8,0},{1,9},{9,1},{2,10},{10,2},{3,11},{11,3},{4,12},{12,4},... | collective-permute-start | bytes 1572872 | tf_op jit(solution)/shard_map/ppermute | solution.py:732
  64.3 15.6 %collective-permute-start.2 = (bf16[256,1024]{1,0:T(8,128)(2,1)}, bf16[256,1024]{1,0:T(8,128)(2,1)S(1)}, u32[]{:S(2)}, u32[]{:S(2)}) collective-permute-start(bf16[256,1024]{1,0:T(8,128)(2,1)} %collective-permute-done.refs_1_.refs_5_), channel_id=1, source_target_pairs={{0,8},{8,0},{1,9},{9,1},{2,10},{10,2},{3,11},{11,3},{4,12},{12,4},... | collective-permute-start | bytes 1572872 | tf_op jit(solution)/shard_map/ppermute | solution.py:732
  97.6 15.5 %collective-permute-start.12 = (bf16[256,1024]{1,0:T(8,128)(2,1)}, bf16[256,1024]{1,0:T(8,128)(2,1)S(1)}, u32[]{:S(2)}, u32[]{:S(2)}) collective-permute-start(bf16[256,1024]{1,0:T(8,128)(2,1)} %get-tuple-element.101), channel_id=1, source_target_pairs={{0,8},{8,0},{1,9},{9,1},{2,10},{10,2},{3,11},{11,3},{4,12},{12,4},... | collective-permute-start | bytes 1572872 | tf_op jit(solution)/shard_map/ppermute | solution.py:732
  106.9 15.7 %collective-permute-start.16 = (bf16[256,1152]{1,0:T(8,128)(2,1)S(1)}, bf16[256,1152]{1,0:T(8,128)(2,1)S(1)}, u32[]{:S(2)}, u32[]{:S(2)}) collective-permute-start(bf16[256,1152]{1,0:T(8,128)(2,1)S(1)} %pad_maximum_fusion.2), channel_id=1, source_target_pairs={{0,1},{1,0},{2,3},{3,2},{4,5},{5,4},{6,7},{7,6},{8,9},{9,8},{10,11... | collective-permute-start | bytes 1769480 | tf_op jit(solution)/shard_map/ppermute | solution.py:732
  109.3 18.0 %collective-permute-start.17 = (bf16[256,1152]{1,0:T(8,128)(2,1)S(1)}, bf16[256,1152]{1,0:T(8,128)(2,1)S(1)}, u32[]{:S(2)}, u32[]{:S(2)}) collective-permute-start(bf16[256,1152]{1,0:T(8,128)(2,1)S(1)} %pad_maximum_fusion.3), channel_id=1, source_target_pairs={{0,16},{16,0},{1,17},{17,1},{2,18},{18,2},{3,19},{19,3},{4,20},{20... | collective-permute-start | bytes 1769480 | tf_op jit(solution)/shard_map/ppermute | solution.py:732
  113.3 24.3 %collective-permute-start.13 = (bf16[256,1024]{1,0:T(8,128)(2,1)S(1)}, bf16[256,1024]{1,0:T(8,128)(2,1)S(1)}, u32[]{:S(2)}, u32[]{:S(2)}) collective-permute-start(bf16[256,1024]{1,0:T(8,128)(2,1)S(1)} %add_convert_fusion.14), channel_id=1, source_target_pairs={{0,16},{16,0},{1,17},{17,1},{2,18},{18,2},{3,19},{19,3},{4,20},{20... | collective-permute-start | bytes 1572872 | tf_op jit(solution)/shard_map/ppermute | solution.py:732
  149.6 20.5 %collective-permute-start.24 = (bf16[512,1152]{1,0:T(8,128)(2,1)}, bf16[512,1152]{1,0:T(8,128)(2,1)}, u32[]{:S(2)}, u32[]{:S(2)}) collective-permute-start(bf16[512,1152]{1,0:T(8,128)(2,1)} %constant_dynamic-update-slice_fusion.5.pack_0), channel_id=1, source_target_pairs={{0,8},{8,0},{1,9},{9,1},{2,10},{10,2},{3,11},{11,3},{4,12},{12,4},... | collective-permute-start | bytes 3538952 | tf_op jit(solution)/shard_map/ppermute | solution.py:732
  149.6 20.5 %collective-permute-start.25 = (bf16[512,1152]{1,0:T(8,128)(2,1)}, bf16[512,1152]{1,0:T(8,128)(2,1)}, u32[]{:S(2)}, u32[]{:S(2)}) collective-permute-start(bf16[512,1152]{1,0:T(8,128)(2,1)} %constant_dynamic-update-slice_fusion.7.pack_1), channel_id=1, source_target_pairs={{0,8},{8,0},{1,9},{9,1},{2,10},{10,2},{3,11},{11,3},{4,12},{12,4},... | collective-permute-start | bytes 3538952 | tf_op jit(solution)/shard_map/ppermute | solution.py:732
  202.6 185.0 %reduce-scatter.6.cloned.1.call-start = ((), (), s32[]{:S(2)}) async-start(), calls=%async_computation.5 | async-start | bytes 2621440 | tf_op jit(solution)/shard_map/reduce_scatter | solution.py:803
  251.8 161.8 %reduce-scatter.8.cloned.1.call-start = ((), (), s32[]{:S(2)}) async-start(), calls=%async_computation.6 | async-start | bytes 2621440 | tf_op jit(solution)/shard_map/reduce_scatter | solution.py:803
  271.3 19.3 %collective-permute-start.33 = (bf16[512,1024]{1,0:T(8,128)(2,1)}, bf16[512,1024]{1,0:T(8,128)(2,1)S(1)}, u32[]{:S(2)}, u32[]{:S(2)}) collective-permute-start(bf16[512,1024]{1,0:T(8,128)(2,1)} %get-tuple-element.129), channel_id=1, source_target_pairs={{0,8},{8,0},{1,9},{9,1},{2,10},{10,2},{3,11},{11,3},{4,12},{12,4},... | collective-permute-start | bytes 3145736 | tf_op jit(solution)/shard_map/ppermute | solution.py:732
  271.3 19.3 %collective-permute-start.38 = (bf16[512,1024]{1,0:T(8,128)(2,1)}, bf16[512,1024]{1,0:T(8,128)(2,1)S(1)}, u32[]{:S(2)}, u32[]{:S(2)}) collective-permute-start(bf16[512,1024]{1,0:T(8,128)(2,1)} %get-tuple-element.133), channel_id=1, source_target_pairs={{0,8},{8,0},{1,9},{9,1},{2,10},{10,2},{3,11},{11,3},{4,12},{12,4},... | collective-permute-start | bytes 3145736 | tf_op jit(solution)/shard_map/ppermute | solution.py:732
  317.7 15.6 %collective-permute-start.39 = (bf16[4,144,512]{2,1,0:T(8,128)(2,1)}, bf16[4,144,512]{2,1,0:T(8,128)(2,1)S(1)}, u32[]{:S(2)}, u32[]{:S(2)}) collective-permute-start(bf16[4,144,512]{2,1,0:T(8,128)(2,1)} %get-tuple-element.144), channel_id=1, source_target_pairs={{0,1},{1,0},{2,3},{3,2},{4,5},{5,4},{6,7},{7,6},{8,9},{9,8},{10,11... | collective-permute-start | bytes 1769480 | tf_op jit(solution)/shard_map/ppermute | solution.py:732
  319.7 15.2 %collective-permute-start.54 = (bf16[128,1024]{1,0:T(8,128)(2,1)S(1)}, bf16[128,1024]{1,0:T(8,128)(2,1)S(1)}, u32[]{:S(2)}, u32[]{:S(2)}) collective-permute-start(bf16[128,1024]{1,0:T(8,128)(2,1)S(1)} %add_convert_fusion.19), channel_id=1, source_target_pairs={{6,0},{8,10},{18,20},{28,30},{7,1},{9,11},{19,21},{29,31}} | collective-permute-start | bytes 786440 | tf_op jit(solution)/shard_map/ppermute | solution.py:988
  320.4 16.6 %collective-permute-start.53 = (bf16[128,1024]{1,0:T(8,128)(2,1)S(1)}, bf16[128,1024]{1,0:T(8,128)(2,1)S(1)}, u32[]{:S(2)}, u32[]{:S(2)}) collective-permute-start(bf16[128,1024]{1,0:T(8,128)(2,1)S(1)} %add_convert_fusion.19), channel_id=1, source_target_pairs={{4,0},{14,10},{16,20},{26,30},{5,1},{15,11},{17,21},{27,31}} | collective-permute-start | bytes 786440 | tf_op jit(solution)/shard_map/ppermute | solution.py:988
  322.2 27.6 %collective-permute-start.52 = (bf16[128,1024]{1,0:T(8,128)(2,1)S(1)}, bf16[128,1024]{1,0:T(8,128)(2,1)S(1)}, u32[]{:S(2)}, u32[]{:S(2)}) collective-permute-start(bf16[128,1024]{1,0:T(8,128)(2,1)S(1)} %add_convert_fusion.19), channel_id=1, source_target_pairs={{2,0},{12,10},{22,20},{24,30},{3,1},{13,11},{23,21},{25,31}} | collective-permute-start | bytes 786440 | tf_op jit(solution)/shard_map/ppermute | solution.py:988
  327.8 52.9 %collective-permute-start.46 = (bf16[256,1024]{1,0:T(8,128)(2,1)S(1)}, bf16[256,1024]{1,0:T(8,128)(2,1)S(1)}, u32[]{:S(2)}, u32[]{:S(2)}) collective-permute-start(bf16[256,1024]{1,0:T(8,128)(2,1)S(1)} %slice.164), channel_id=1, source_target_pairs={{0,16},{16,0},{1,17},{17,1},{2,18},{18,2},{3,19},{19,3},{4,20},{20... | collective-permute-start | bytes 1572872 | tf_op jit(solution)/shard_map/ppermute | solution.py:732
  333.3 49.0 %collective-permute-start.34 = (bf16[256,1024]{1,0:T(8,128)(2,1)S(1)}, bf16[256,1024]{1,0:T(8,128)(2,1)S(1)}, u32[]{:S(2)}, u32[]{:S(2)}) collective-permute-start(bf16[256,1024]{1,0:T(8,128)(2,1)S(1)} %slice.160), channel_id=1, source_target_pairs={{0,1},{1,0},{2,3},{3,2},{4,5},{5,4},{6,7},{7,6},{8,9},{9,8},{10,11... | collective-permute-start | bytes 1572872 | tf_op jit(solution)/shard_map/ppermute | solution.py:732
  335.0 27.7 %collective-permute-start.44 = (bf16[144,512]{1,0:T(8,128)(2,1)S(1)}, bf16[144,512]{1,0:T(8,128)(2,1)S(1)}, u32[]{:S(2)}, u32[]{:S(2)}) collective-permute-start(bf16[144,512]{1,0:T(8,128)(2,1)S(1)} %get-tuple-element.195), channel_id=1, source_target_pairs={{0,2},{2,4},{4,6},{6,0},{1,3},{3,5},{5,7},{7,1},{8,10},{10,12},{12... | collective-permute-start | bytes 442376 | tf_op jit(solution)/shard_map/ppermute | solution.py:732
  337.0 25.7 %collective-permute-start.43 = (bf16[144,512]{1,0:T(8,128)(2,1)S(1)}, bf16[144,512]{1,0:T(8,128)(2,1)S(1)}, u32[]{:S(2)}, u32[]{:S(2)}) collective-permute-start(bf16[144,512]{1,0:T(8,128)(2,1)S(1)} %get-tuple-element.196), channel_id=1, source_target_pairs={{0,4},{2,6},{4,0},{6,2},{1,5},{3,7},{5,1},{7,3},{8,12},{10,14},{12... | collective-permute-start | bytes 442376 | tf_op jit(solution)/shard_map/ppermute | solution.py:732
  349.8 30.8 %collective-permute-start.42 = (bf16[144,512]{1,0:T(8,128)(2,1)S(1)}, bf16[144,512]{1,0:T(8,128)(2,1)S(1)}, u32[]{:S(2)}, u32[]{:S(2)}) collective-permute-start(bf16[144,512]{1,0:T(8,128)(2,1)S(1)} %get-tuple-element.194), channel_id=1, source_target_pairs={{0,6},{2,0},{4,2},{6,4},{1,7},{3,1},{5,3},{7,5},{8,14},{10,8},{12,... | collective-permute-start | bytes 442376 | tf_op jit(solution)/shard_map/ppermute | solution.py:732
  384.8 15.6 %collective-permute-start.56 = (bf16[128,1024]{1,0:T(8,128)(2,1)}, bf16[128,1024]{1,0:T(8,128)(2,1)}, u32[]{:S(2)}, u32[]{:S(2)}) collective-permute-start(bf16[128,1024]{1,0:T(8,128)(2,1)} %add_convert_fusion.16), channel_id=1, source_target_pairs={{0,16},{10,26},{20,4},{30,14},{1,17},{11,27},{21,5},{31,15}} | collective-permute-start | bytes 786440 | tf_op jit(solution)/shard_map/ppermute | solution.py:998
  (95 other events, 1182.4 us)
Sparse Core Ops, SparseCore 0:
  10.2 65.5 all-gather.7
  77.9 45.9 all-gather.9
  125.5 44.6 all-gather.5
  202.7 41.9 reduce-scatter.3
  251.9 42.0 reduce-scatter.5
  317.8 66.9 reduce-scatter.7

commit v3 on v2

--- a/solution.py
+++ b/solution.py
@@ -986,7 +986,7 @@
     out_total = out_piece.astype(high)
     for moves in diagonal_moves(False):
         moved = lax.ppermute(out_piece, joint, [(b, a) for a, b in moves])
-        out_total = out_total + after(moved, qkv_sum).astype(high)
+        out_total = out_total + after(moved, qkv_total).astype(high)
     out_piece = out_total.astype(low)
     norm_one_grad = norm_one_low.astype(high)
     input_grad = middle_grad + norm_back(inputs, scale_one, gain_one, norm_one_grad)

time: 437 us -> 433 us (level)
  the two profiles are of different devices: /device:TPU:8 before, /device:TPU:0 now
where the time goes in v3:
time: 433 us; the launch traced here: 426 us
  Pallas kernels  127 us (29%)
  waiting for transfers between devices  124 us (29%)
  starting transfers between devices  90.2 us (21%)
  other arithmetic  47.4 us (11%)
  local copies, waits for them, and re-layouts  21.8 us (5%)
  between operations  15.5 us (4%)
    ppermute x49, waiting for transfers between devices, shifted(): lax.ppermute(value, axis, [(j, (j + step) % size) for j in range(size)])  87.8 us
    ppermute x49, starting transfers between devices, shifted(): lax.ppermute(value, axis, [(j, (j + step) % size) for j in range(size)])  63.9 us
    pallas_call x1, Pallas kernels, run_experts(): pl.pallas_call(experts_kernel, grid=(len(h_all),), out_shape=(jax.ShapeDt...  32.4 us
    pallas_call x1, Pallas kernels, attend_back(): pl.pallas_call(functools.partial(attend_back_kernel, count, heads, keys,...  19.5 us
    ppermute x3, starting transfers between devices, body(): out_all = out_all + lax.ppermute(out_pair, joint, moves)  18 us
    ppermute x3, waiting for transfers between devices, body(): moved = lax.ppermute(out_piece, joint, [(b, a) for a, b in moves])  17.6 us
    pallas_call x2, Pallas kernels, weight_grads(): pl.pallas_call(weight_grads_kernel, grid=(owned,), out_shape=(jax.ShapeDt...  17.4 us
    pallas_call x1, Pallas kernels, back_rows(): pl.pallas_call(back_rows_kernel, grid=(4,), out_shape=(jax.ShapeDtypeStru...  16.6 us
  transfers between devices with their start and end apart: 64, of which 28 were waited for; matrix products, arithmetic and copies ran while one was open for 14% of the time, Pallas kernels for 21%

profile of v3, /device:TPU:0, one launch (start us, length us, event | category | flops | bytes accessed | tf_op | source)
XLA Modules:
  0.0 425.8 jit_solution(7862167576149718723)
XLA Ops:
  13.4 3.0 collective-permute-start.3
  30.0 6.4 %collective-permute-done.4 = bf16[144,512]{1,0:T(8,128)(2,1)} collective-permute-done((bf16[144,512]{1,0:T(8,128)(2,1)}, bf16[144,512]{1,0:T(8,128)(2,1)}, u32[]{:S(2)}, u32[]{:S(2)}) %collective-permute-start.4) | collective-permute-done | bytes 147488 | tf_op jit(solution)/shard_map/ppermute | solution.py:732
  43.0 12.9 %collective-permute-start.10 = (bf16[256,1024]{1,0:T(8,128)(2,1)S(1)}, bf16[256,1024]{1,0:T(8,128)(2,1)}, u32[]{:S(2)}, u32[]{:S(2)}) collective-permute-start(bf16[256,1024]{1,0:T(8,128)(2,1)S(1)} %pad_maximum_fusion.7), channel_id=1, source_target_pairs={{0,6},{10,8},{20,18},{30,28},{1,7},{11,9},{21,19},{31,29}} | collective-permute-start | bytes 1572872 | tf_op jit(solution)/shard_map/ppermute | solution.py:894
  61.9 3.9 collective-permute-done.10
  68.4 3.0 collective-permute-done.9
  72.9 4.1 collective-permute-done.8
  81.3 13.9 %attend.1 = (bf16[1024,1024]{1,0:T(8,128)(2,1)}, bf16[1024,512]{1,0:T(8,128)(2,1)}, bf16[32,1024]{1,0:T(8,128)(2,1)}, bf16[4,1024,64]{2,1,0:T(8,128)(2,1)}, bf16...) custom-call(s32[4]{0:T(128)} %fusion.33.blocks, ...), custom_call_target="tpu_custom_call" | custom-call | tf_op jit(solution)/shard_map/attend/pallas_call | solution.py:171
  102.3 16.2 %collective-permute-start.17 = (bf16[256,1152]{1,0:T(8,128)(2,1)S(1)}, bf16[256,1152]{1,0:T(8,128)(2,1)S(1)}, u32[]{:S(2)}, u32[]{:S(2)}) collective-permute-start(bf16[256,1152]{1,0:T(8,128)(2,1)S(1)} %pad_maximum_fusion.3), channel_id=1, source_target_pairs={{0,16},{16,0},{1,17},{17,1},{2,18},{18,2},{3,19},{19,3},{4,20},{20... | collective-permute-start | bytes 1769480 | tf_op jit(solution)/shard_map/ppermute | solution.py:732
  120.6 12.1 %collective-permute-done.17 = bf16[256,1152]{1,0:T(8,128)(2,1)S(1)} collective-permute-done((bf16[256,1152]{1,0:T(8,128)(2,1)S(1)}, bf16[256,1152]{1,0:T(8,128)(2,1)S(1)}, u32[]{:S(2)}, u32[]{:S(2)}) %collective-permute-start.17) | collective-permute-done | bytes 589856 | tf_op jit(solution)/shard_map/ppermute | solution.py:732
  133.6 9.5 %collective-permute-done.13 = bf16[256,1024]{1,0:T(8,128)(2,1)S(1)} collective-permute-done((bf16[256,1024]{1,0:T(8,128)(2,1)S(1)}, bf16[256,1024]{1,0:T(8,128)(2,1)S(1)}, u32[]{:S(2)}, u32[]{:S(2)}) %collective-permute-start.13) | collective-permute-done | bytes 524320 | tf_op jit(solution)/shard_map/ppermute | solution.py:732
  146.3 5.3 %collective-permute-done.18 = bf16[128,1024]{1,0:T(8,128)(2,1)S(1)} collective-permute-done((bf16[128,1024]{1,0:T(8,128)(2,1)S(1)}, bf16[128,1024]{1,0:T(8,128)(2,1)S(1)}, u32[]{:S(2)}, u32[]{:S(2)}) %collective-permute-start.18) | collective-permute-done | bytes 262176 | tf_op jit(solution)/shard_map/ppermute | solution.py:732
  157.8 7.9 %collective-permute-done.20 = bf16[256,1024]{1,0:T(8,128)(2,1)S(1)} collective-permute-done((bf16[256,1024]{1,0:T(8,128)(2,1)}, bf16[256,1024]{1,0:T(8,128)(2,1)S(1)}, u32[]{:S(2)}, u32[]{:S(2)}) %collective-permute-start.20) | collective-permute-done | bytes 524320 | tf_op jit(solution)/shard_map/ppermute | solution.py:732
  167.1 6.2 %all-gather.6.cloned.1.call-done.down_ref = bf16[4,256,1024]{2,1,0:T(8,128)(2,1)} async-done(((bf16[4,64,1024]{2,1,0:T(8,128)(2,1)}), bf16[4,256,1024]{2,1,0:T(8,128)(2,1)}) %all-gather.6.cloned.1.call-update) | async-done | bytes 2097168 | tf_op jit(solution)/shard_map/all_gather | solution.py:799
  173.4 32.4 %experts.1 = (bf16[2048,1024]{1,0:T(8,128)(2,1)}, bf16[2048,1024]{1,0:T(8,128)(2,1)}, bf16[2048,1024]{1,0:T(8,128)(2,1)}, bf16[2048,16]{1,0:T(8,128)(2,1)}, f32[...) custom-call(s32[1]{0:T(128)} %bitcast.10.first, bf16[512,1024]{1,0:T(8,128)(2,1)} %copy-done.4, ...), custom_call_target="tpu_custom_call" | custom-call | tf_op jit(solution)/shard_map/experts/pallas_call | solution.py:315
  205.9 16.6 %back_rows.1 = (bf16[512,1024]{1,0:T(8,128)(2,1)}, bf16[512,1024]{1,0:T(8,128)(2,1)}, bf16[512,1024]{1,0:T(8,128)(2,1)}, bf16[512,1024]{1,0:T(8,128)(2,1)}) custom-call(bf16[2048,1024]{1,0:T(8,128)(2,1)} %get-tuple-element.117.gate_grad_ref.grad_ref, bf16[2048,1024]{1,0:T(8,128)(2,1)} %get-tuple-element.120.up_grad_ref.grad_ref, ...), custom_call_target="tpu_custom_call" | custom-call | tf_op jit(solution)/shard_map/back_rows/pallas_call | solution.py:371
  223.0 8.7 %weight_grads.2 = bf16[4,256,1024]{2,1,0:T(8,128)(2,1)} custom-call(bf16[2048,1024]{1,0:T(8,128)(2,1)} %get-tuple-element.117.gate_grad_ref.grad_ref, bf16[512,1024]{1,0:T(8,128)(2,1)} %copy-done.4, bf16[512,1024]{1,0:T(8,128)(2,1)} %copy-done.3, bf16[512,1024]{1,0:T(8,128)(2,1)} %collective-permute-done.22.h_2, bf16[512,1024]{1,0:T(8,128)(2,1)} %collective-permute-done.23.h_3), custom_call_target="tpu_custom_call" | custom-call | tf_op jit(solution)/shard_map/weight_grads/pallas_call | solution.py:407
  239.6 8.7 %weight_grads.3 = bf16[4,256,1024]{2,1,0:T(8,128)(2,1)} custom-call(bf16[2048,1024]{1,0:T(8,128)(2,1)} %get-tuple-element.120.up_grad_ref.grad_ref, bf16[512,1024]{1,0:T(8,128)(2,1)} %copy-done.4, bf16[512,1024]{1,0:T(8,128)(2,1)} %copy-done.3, bf16[512,1024]{1,0:T(8,128)(2,1)} %collective-permute-done.22.h_2, bf16[512,1024]{1,0:T(8,128)(2,1)} %collective-permute-done.23.h_3), custom_call_target="tpu_custom_call" | custom-call | tf_op jit(solution)/shard_map/weight_grads/pallas_call | solution.py:407
  257.5 3.6 collective-permute-done.29
  264.1 9.6 %expert_results.1 = (bf16[512,1024]{1,0:T(8,128)(2,1)}, bf16[512,1024]{1,0:T(8,128)(2,1)}, bf16[512,1024]{1,0:T(8,128)(2,1)}, bf16[512,1024]{1,0:T(8,128)(2,1)}) custom-call(bf16[2048,1024]{1,0:T(8,128)(2,1)} %get-tuple-element.123.act_ref, bf16[1024,1024]{1,0:T(8,128)(2,1)} %bitcast.69), custom_call_target="tpu_custom_call" | custom-call | tf_op jit(solution)/shard_map/expert_results/pallas_call | solution.py:432
  275.4 3.1 collective-permute-done.35.refs_2_
  280.9 3.3 out_grads.1
  286.1 6.6 %collective-permute-done.37 = bf16[128,1024]{1,0:T(8,128)(2,1)S(1)} collective-permute-done((bf16[128,1024]{1,0:T(8,128)(2,1)}, bf16[128,1024]{1,0:T(8,128)(2,1)S(1)}, u32[]{:S(2)}, u32[]{:S(2)}) %collective-permute-start.37) | collective-permute-done | bytes 262176 | tf_op jit(solution)/shard_map/ppermute | solution.py:732
  297.0 4.3 %multiply_subtract_fusion = (f32[4,64,1024]{2,1,0:T(8,128)}, f32[4,64,1024]{2,1,0:T(8,128)}, f32[4,64,1024]{2,1,0:T(8,128)}) fusion(f32[4,64,1024]{2,1,0:T(8,128)} %param.39, bf16[4,64,1024]{2,1,0:T(8,128)(2,1)} %reduce-scatter.4.cloned.1.call-done, f32[4,64,1024]{2,1,0:T(8,128)} %param.41, f32[4,64,1024]{2,1,0:T(8,128)} %param.40), kind=kLoop, calls=%fused_computation.29 | loop fusion | flops 4194304 | bytes 6815744 | tf_op jit(solution)/shard_map/sub | solution.py:68
  301.4 19.5 %attend_back.1 = (bf16[4,144,512]{2,1,0:T(8,128)(2,1)}, bf16[4,144,512]{2,1,0:T(8,128)(2,1)}, bf16[256,1024]{1,0:T(8,128)(2,1)}, bf16[256,1024]{1,0:T(8,128)(2,1...) custom-call(s32[4]{0:T(128)} %fusion.33.blocks, s32[8]{0:T(128)} %fusion.35.shard_at, ...), custom_call_target="tpu_custom_call" | custom-call | tf_op jit(solution)/shard_map/attend_back/pallas_call | solution.py:608
  329.3 8.6 %collective-permute-done.39 = bf16[4,144,512]{2,1,0:T(8,128)(2,1)S(1)} collective-permute-done((bf16[4,144,512]{2,1,0:T(8,128)(2,1)}, bf16[4,144,512]{2,1,0:T(8,128)(2,1)S(1)}, u32[]{:S(2)}, u32[]{:S(2)}) %collective-permute-start.39) | collective-permute-done | bytes 589856 | tf_op jit(solution)/shard_map/ppermute | solution.py:732
  342.9 7.2 %collective-permute-done.44 = bf16[144,512]{1,0:T(8,128)(2,1)S(1)} collective-permute-done((bf16[144,512]{1,0:T(8,128)(2,1)S(1)}, bf16[144,512]{1,0:T(8,128)(2,1)S(1)}, u32[]{:S(2)}, u32[]{:S(2)}) %collective-permute-start.44) | collective-permute-done | bytes 147488 | tf_op jit(solution)/shard_map/ppermute | solution.py:732
  351.6 7.6 %collective-permute-done.43 = bf16[144,512]{1,0:T(8,128)(2,1)S(1)} collective-permute-done((bf16[144,512]{1,0:T(8,128)(2,1)S(1)}, bf16[144,512]{1,0:T(8,128)(2,1)S(1)}, u32[]{:S(2)}, u32[]{:S(2)}) %collective-permute-start.43) | collective-permute-done | bytes 147488 | tf_op jit(solution)/shard_map/ppermute | solution.py:732
  364.5 5.0 %collective-permute-start.45 = (bf16[128,1024]{1,0:T(8,128)(2,1)S(1)}, bf16[128,1024]{1,0:T(8,128)(2,1)S(1)}, u32[]{:S(2)}, u32[]{:S(2)}) collective-permute-start(bf16[128,1024]{1,0:T(8,128)(2,1)S(1)} %slice.162), channel_id=1, source_target_pairs={{0,16},{16,0},{1,17},{17,1},{2,18},{18,2},{3,19},{19,3},{4,20},{20... | collective-permute-start | bytes 786440 | tf_op jit(solution)/shard_map/ppermute | solution.py:732
  370.8 16.2 %collective-permute-done.53 = bf16[128,1024]{1,0:T(8,128)(2,1)} collective-permute-done((bf16[128,1024]{1,0:T(8,128)(2,1)}, bf16[128,1024]{1,0:T(8,128)(2,1)}, u32[]{:S(2)}, u32[]{:S(2)}) %collective-permute-start.53) | collective-permute-done | bytes 262176 | tf_op jit(solution)/shard_map/ppermute | solution.py:988
  397.4 4.8 %qkv_step.1 = (f32[128,2048]{1,0:T(8,128)}, f32[128,2048]{1,0:T(8,128)}, f32[128,2048]{1,0:T(8,128)}, f32[16,512]{1,0:T(8,128)}) custom-call(s32[4]{0:T(128)} %fusion.36.slots, bf16[4,144,512]{2,1,0:T(8,128)(2,1)} %pad_maximum_fusion.4.g_ref, f32[128,2048]{1,0:T(8,128)} %w_ref.2, f32[128,2048]{1,0:T(8,128)} %m_ref.2, f32[128,2048]{1,0:T(8,128)} %v_ref.2), custom_call_target="tpu_custom_call" | custom-call | tf_op jit(solution)/shard_map/qkv_step/pallas_call | solution.py:686
  406.4 3.3 collective-permute-done.48
  410.1 6.6 %in_step.1 = (f32[4,2,64,1024]{3,2,1,0:T(8,128)}, f32[4,2,64,1024]{3,2,1,0:T(8,128)}, f32[4,2,64,1024]{3,2,1,0:T(8,128)}) custom-call(bf16[4,64,1024]{2,1,0:T(8,128)(2,1)} %reduce-scatter.6.cloned.1.call-done.gate_ref, bf16[4,64,1024]{2,1,0:T(8,128)(2,1)} %reduce-scatter.8.cloned.1.call-done.up_ref, f32[4,2,64,1024]{3,2,1,0:T(8,128)} %w_ref.3, ...), custom_call_target="tpu_custom_call" | custom-call | tf_op jit(solution)/shard_map/in_step/pallas_call | solution.py:718
  (325 shorter events, 130.3 us)
Async XLA Ops:
  7.2 88.0 %all-gather.8.cloned.1.call-start = ((), (), s32[]{:S(2)}) async-start(), calls=%async_computation.7 | async-start | bytes 2621440 | tf_op jit(solution)/shard_map/all_gather | solution.py:799
  10.0 143.6 %all-gather.10.cloned.1.call-start = ((), (), s32[]{:S(2)}) async-start(), calls=%async_computation.8 | async-start | bytes 2621440 | tf_op jit(solution)/shard_map/all_gather | solution.py:799
  10.7 162.6 %all-gather.6.cloned.1.call-start = ((), (), s32[]{:S(2)}) async-start(), calls=%async_computation.3 | async-start | bytes 2621440 | tf_op jit(solution)/shard_map/all_gather | solution.py:799
  16.4 20.0 %collective-permute-start.4 = (bf16[144,512]{1,0:T(8,128)(2,1)}, bf16[144,512]{1,0:T(8,128)(2,1)}, u32[]{:S(2)}, u32[]{:S(2)}) collective-permute-start(bf16[144,512]{1,0:T(8,128)(2,1)} %get-tuple-element.187), channel_id=1, source_target_pairs={{0,4},{2,6},{4,0},{6,2},{1,5},{3,7},{5,1},{7,3},{8,12},{10,14},{12... | collective-permute-start | bytes 442376 | tf_op jit(solution)/shard_map/ppermute | solution.py:732
  20.3 41.5 %collective-permute-start = (bf16[256,1024]{1,0:T(8,128)(2,1)S(1)}, bf16[256,1024]{1,0:T(8,128)(2,1)}, u32[]{:S(2)}, u32[]{:S(2)}) collective-permute-start(bf16[256,1024]{1,0:T(8,128)(2,1)S(1)} %bitcast.67), channel_id=1, source_target_pairs={{0,16},{16,0},{1,17},{17,1},{2,18},{18,2},{3,19},{19,3},{4,20},{20... | collective-permute-start | bytes 1572872 | tf_op jit(solution)/shard_map/ppermute | solution.py:732
  21.9 20.1 %collective-permute-start.7 = (bf16[128,1024]{1,0:T(8,128)(2,1)S(1)}, bf16[128,1024]{1,0:T(8,128)(2,1)}, u32[]{:S(2)}, u32[]{:S(2)}) collective-permute-start(bf16[128,1024]{1,0:T(8,128)(2,1)S(1)} %convert_element_type.294), channel_id=1, source_target_pairs={{0,1},{1,0},{2,3},{3,2},{4,5},{5,4},{6,7},{7,6},{8,9},{9,8},{10,11... | collective-permute-start | bytes 786440 | tf_op jit(solution)/shard_map/ppermute | solution.py:732
  24.4 272.7 %reduce-scatter.4.cloned.1.call-start = ((), (), s32[]{:S(2)}) async-start(), calls=%async_computation.4 | async-start | bytes 2621440 | tf_op jit(solution)/shard_map/reduce_scatter | solution.py:803
  37.6 23.4 %collective-permute-start.6 = (bf16[4,144,512]{2,1,0:T(8,128)(2,1)S(1)}, bf16[4,144,512]{2,1,0:T(8,128)(2,1)S(1)}, u32[]{:S(2)}, u32[]{:S(2)}) collective-permute-start(bf16[4,144,512]{2,1,0:T(8,128)(2,1)S(1)} %pad_maximum_fusion), channel_id=1, source_target_pairs={{0,1},{1,0},{2,3},{3,2},{4,5},{5,4},{6,7},{7,6},{8,9},{9,8},{10,11... | collective-permute-start | bytes 1769480 | tf_op jit(solution)/shard_map/ppermute | solution.py:732
  43.0 22.8 %collective-permute-start.10 = (bf16[256,1024]{1,0:T(8,128)(2,1)S(1)}, bf16[256,1024]{1,0:T(8,128)(2,1)}, u32[]{:S(2)}, u32[]{:S(2)}) collective-permute-start(bf16[256,1024]{1,0:T(8,128)(2,1)S(1)} %pad_maximum_fusion.7), channel_id=1, source_target_pairs={{0,6},{10,8},{20,18},{30,28},{1,7},{11,9},{21,19},{31,29}} | collective-permute-start | bytes 1572872 | tf_op jit(solution)/shard_map/ppermute | solution.py:894
  58.2 18.7 %collective-permute-start.8 = (bf16[256,1024]{1,0:T(8,128)(2,1)S(1)}, bf16[256,1024]{1,0:T(8,128)(2,1)}, u32[]{:S(2)}, u32[]{:S(2)}) collective-permute-start(bf16[256,1024]{1,0:T(8,128)(2,1)S(1)} %pad_maximum_fusion.7), channel_id=1, source_target_pairs={{0,2},{10,12},{20,22},{30,24},{1,3},{11,13},{21,23},{31,25}} | collective-permute-start | bytes 1572872 | tf_op jit(solution)/shard_map/ppermute | solution.py:894
  61.9 18.4 %collective-permute-start.1 = (bf16[256,1024]{1,0:T(8,128)(2,1)S(1)}, bf16[256,1024]{1,0:T(8,128)(2,1)S(1)}, u32[]{:S(2)}, u32[]{:S(2)}) collective-permute-start(bf16[256,1024]{1,0:T(8,128)(2,1)S(1)} %bitcast.68), channel_id=1, source_target_pairs={{0,8},{8,0},{1,9},{9,1},{2,10},{10,2},{3,11},{11,3},{4,12},{12,4},... | collective-permute-start | bytes 1572872 | tf_op jit(solution)/shard_map/ppermute | solution.py:732
  98.0 20.5 %collective-permute-start.12 = (bf16[256,1024]{1,0:T(8,128)(2,1)}, bf16[256,1024]{1,0:T(8,128)(2,1)S(1)}, u32[]{:S(2)}, u32[]{:S(2)}) collective-permute-start(bf16[256,1024]{1,0:T(8,128)(2,1)} %get-tuple-element.101), channel_id=1, source_target_pairs={{0,8},{8,0},{1,9},{9,1},{2,10},{10,2},{3,11},{11,3},{4,12},{12,4},... | collective-permute-start | bytes 1572872 | tf_op jit(solution)/shard_map/ppermute | solution.py:732
  99.4 20.3 %collective-permute-start.11 = (bf16[256,1024]{1,0:T(8,128)(2,1)}, bf16[256,1024]{1,0:T(8,128)(2,1)S(1)}, u32[]{:S(2)}, u32[]{:S(2)}) collective-permute-start(bf16[256,1024]{1,0:T(8,128)(2,1)} %get-tuple-element.99), channel_id=1, source_target_pairs={{0,8},{8,0},{1,9},{9,1},{2,10},{10,2},{3,11},{11,3},{4,12},{12,4},... | collective-permute-start | bytes 1572872 | tf_op jit(solution)/shard_map/ppermute | solution.py:732
  99.9 19.8 %collective-permute-start.16 = (bf16[256,1152]{1,0:T(8,128)(2,1)S(1)}, bf16[256,1152]{1,0:T(8,128)(2,1)S(1)}, u32[]{:S(2)}, u32[]{:S(2)}) collective-permute-start(bf16[256,1152]{1,0:T(8,128)(2,1)S(1)} %pad_maximum_fusion.2), channel_id=1, source_target_pairs={{0,1},{1,0},{2,3},{3,2},{4,5},{5,4},{6,7},{7,6},{8,9},{9,8},{10,11... | collective-permute-start | bytes 1769480 | tf_op jit(solution)/shard_map/ppermute | solution.py:732
  102.3 30.4 %collective-permute-start.17 = (bf16[256,1152]{1,0:T(8,128)(2,1)S(1)}, bf16[256,1152]{1,0:T(8,128)(2,1)S(1)}, u32[]{:S(2)}, u32[]{:S(2)}) collective-permute-start(bf16[256,1152]{1,0:T(8,128)(2,1)S(1)} %pad_maximum_fusion.3), channel_id=1, source_target_pairs={{0,16},{16,0},{1,17},{17,1},{2,18},{18,2},{3,19},{19,3},{4,20},{20... | collective-permute-start | bytes 1769480 | tf_op jit(solution)/shard_map/ppermute | solution.py:732
  118.7 24.3 %collective-permute-start.13 = (bf16[256,1024]{1,0:T(8,128)(2,1)S(1)}, bf16[256,1024]{1,0:T(8,128)(2,1)S(1)}, u32[]{:S(2)}, u32[]{:S(2)}) collective-permute-start(bf16[256,1024]{1,0:T(8,128)(2,1)S(1)} %add_convert_fusion.14), channel_id=1, source_target_pairs={{0,16},{16,0},{1,17},{17,1},{2,18},{18,2},{3,19},{19,3},{4,20},{20... | collective-permute-start | bytes 1572872 | tf_op jit(solution)/shard_map/ppermute | solution.py:732
  155.1 18.2 %collective-permute-start.24 = (bf16[512,1152]{1,0:T(8,128)(2,1)}, bf16[512,1152]{1,0:T(8,128)(2,1)}, u32[]{:S(2)}, u32[]{:S(2)}) collective-permute-start(bf16[512,1152]{1,0:T(8,128)(2,1)} %constant_dynamic-update-slice_fusion.5.pack_0), channel_id=1, source_target_pairs={{0,8},{8,0},{1,9},{9,1},{2,10},{10,2},{3,11},{11,3},{4,12},{12,4},... | collective-permute-start | bytes 3538952 | tf_op jit(solution)/shard_map/ppermute | solution.py:732
  155.1 18.2 %collective-permute-start.25 = (bf16[512,1152]{1,0:T(8,128)(2,1)}, bf16[512,1152]{1,0:T(8,128)(2,1)}, u32[]{:S(2)}, u32[]{:S(2)}) collective-permute-start(bf16[512,1152]{1,0:T(8,128)(2,1)} %constant_dynamic-update-slice_fusion.7.pack_1), channel_id=1, source_target_pairs={{0,8},{8,0},{1,9},{9,1},{2,10},{10,2},{3,11},{11,3},{4,12},{12,4},... | collective-permute-start | bytes 3538952 | tf_op jit(solution)/shard_map/ppermute | solution.py:732
  205.8 163.7 %reduce-scatter.6.cloned.1.call-start = ((), (), s32[]{:S(2)}) async-start(), calls=%async_computation.5 | async-start | bytes 2621440 | tf_op jit(solution)/shard_map/reduce_scatter | solution.py:803
  254.9 155.2 %reduce-scatter.8.cloned.1.call-start = ((), (), s32[]{:S(2)}) async-start(), calls=%async_computation.6 | async-start | bytes 2621440 | tf_op jit(solution)/shard_map/reduce_scatter | solution.py:803
  274.4 20.0 %collective-permute-start.33 = (bf16[512,1024]{1,0:T(8,128)(2,1)}, bf16[512,1024]{1,0:T(8,128)(2,1)S(1)}, u32[]{:S(2)}, u32[]{:S(2)}) collective-permute-start(bf16[512,1024]{1,0:T(8,128)(2,1)} %get-tuple-element.129), channel_id=1, source_target_pairs={{0,8},{8,0},{1,9},{9,1},{2,10},{10,2},{3,11},{11,3},{4,12},{12,4},... | collective-permute-start | bytes 3145736 | tf_op jit(solution)/shard_map/ppermute | solution.py:732
  274.4 20.0 %collective-permute-start.38 = (bf16[512,1024]{1,0:T(8,128)(2,1)}, bf16[512,1024]{1,0:T(8,128)(2,1)S(1)}, u32[]{:S(2)}, u32[]{:S(2)}) collective-permute-start(bf16[512,1024]{1,0:T(8,128)(2,1)} %get-tuple-element.133), channel_id=1, source_target_pairs={{0,8},{8,0},{1,9},{9,1},{2,10},{10,2},{3,11},{11,3},{4,12},{12,4},... | collective-permute-start | bytes 3145736 | tf_op jit(solution)/shard_map/ppermute | solution.py:732
  324.6 37.2 %collective-permute-start.46 = (bf16[256,1024]{1,0:T(8,128)(2,1)S(1)}, bf16[256,1024]{1,0:T(8,128)(2,1)S(1)}, u32[]{:S(2)}, u32[]{:S(2)}) collective-permute-start(bf16[256,1024]{1,0:T(8,128)(2,1)S(1)} %slice.164), channel_id=1, source_target_pairs={{0,16},{16,0},{1,17},{17,1},{2,18},{18,2},{3,19},{19,3},{4,20},{20... | collective-permute-start | bytes 1572872 | tf_op jit(solution)/shard_map/ppermute | solution.py:732
  326.4 37.9 %collective-permute-start.34 = (bf16[256,1024]{1,0:T(8,128)(2,1)S(1)}, bf16[256,1024]{1,0:T(8,128)(2,1)S(1)}, u32[]{:S(2)}, u32[]{:S(2)}) collective-permute-start(bf16[256,1024]{1,0:T(8,128)(2,1)S(1)} %slice.160), channel_id=1, source_target_pairs={{0,1},{1,0},{2,3},{3,2},{4,5},{5,4},{6,7},{7,6},{8,9},{9,8},{10,11... | collective-permute-start | bytes 1572872 | tf_op jit(solution)/shard_map/ppermute | solution.py:732
  338.2 20.9 %collective-permute-start.43 = (bf16[144,512]{1,0:T(8,128)(2,1)S(1)}, bf16[144,512]{1,0:T(8,128)(2,1)S(1)}, u32[]{:S(2)}, u32[]{:S(2)}) collective-permute-start(bf16[144,512]{1,0:T(8,128)(2,1)S(1)} %get-tuple-element.196), channel_id=1, source_target_pairs={{0,4},{2,6},{4,0},{6,2},{1,5},{3,7},{5,1},{7,3},{8,12},{10,14},{12... | collective-permute-start | bytes 442376 | tf_op jit(solution)/shard_map/ppermute | solution.py:732
  340.0 20.4 %collective-permute-start.42 = (bf16[144,512]{1,0:T(8,128)(2,1)S(1)}, bf16[144,512]{1,0:T(8,128)(2,1)S(1)}, u32[]{:S(2)}, u32[]{:S(2)}) collective-permute-start(bf16[144,512]{1,0:T(8,128)(2,1)S(1)} %get-tuple-element.194), channel_id=1, source_target_pairs={{0,6},{2,0},{4,2},{6,4},{1,7},{3,1},{5,3},{7,5},{8,14},{10,8},{12,... | collective-permute-start | bytes 442376 | tf_op jit(solution)/shard_map/ppermute | solution.py:732
  350.1 20.8 %collective-permute-start.54 = (bf16[128,1024]{1,0:T(8,128)(2,1)}, bf16[128,1024]{1,0:T(8,128)(2,1)}, u32[]{:S(2)}, u32[]{:S(2)}) collective-permute-start(bf16[128,1024]{1,0:T(8,128)(2,1)} %add_convert_fusion.19), channel_id=1, source_target_pairs={{6,0},{8,10},{18,20},{28,30},{7,1},{9,11},{19,21},{29,31}} | collective-permute-start | bytes 786440 | tf_op jit(solution)/shard_map/ppermute | solution.py:988
  359.1 27.9 %collective-permute-start.53 = (bf16[128,1024]{1,0:T(8,128)(2,1)}, bf16[128,1024]{1,0:T(8,128)(2,1)}, u32[]{:S(2)}, u32[]{:S(2)}) collective-permute-start(bf16[128,1024]{1,0:T(8,128)(2,1)} %add_convert_fusion.19), channel_id=1, source_target_pairs={{4,0},{14,10},{16,20},{26,30},{5,1},{15,11},{17,21},{27,31}} | collective-permute-start | bytes 786440 | tf_op jit(solution)/shard_map/ppermute | solution.py:988
  360.4 26.7 %collective-permute-start.52 = (bf16[128,1024]{1,0:T(8,128)(2,1)}, bf16[128,1024]{1,0:T(8,128)(2,1)}, u32[]{:S(2)}, u32[]{:S(2)}) collective-permute-start(bf16[128,1024]{1,0:T(8,128)(2,1)} %add_convert_fusion.19), channel_id=1, source_target_pairs={{2,0},{12,10},{22,20},{24,30},{3,1},{13,11},{23,21},{25,31}} | collective-permute-start | bytes 786440 | tf_op jit(solution)/shard_map/ppermute | solution.py:988
  362.8 28.3 %collective-permute-start.47 = (bf16[128,1024]{1,0:T(8,128)(2,1)}, bf16[128,1024]{1,0:T(8,128)(2,1)}, u32[]{:S(2)}, u32[]{:S(2)}) collective-permute-start(bf16[128,1024]{1,0:T(8,128)(2,1)} %slice.166), channel_id=1, source_target_pairs={{0,1},{1,0},{2,3},{3,2},{4,5},{5,4},{6,7},{7,6},{8,9},{9,8},{10,11... | collective-permute-start | bytes 786440 | tf_op jit(solution)/shard_map/ppermute | solution.py:732
  364.5 29.6 %collective-permute-start.45 = (bf16[128,1024]{1,0:T(8,128)(2,1)S(1)}, bf16[128,1024]{1,0:T(8,128)(2,1)S(1)}, u32[]{:S(2)}, u32[]{:S(2)}) collective-permute-start(bf16[128,1024]{1,0:T(8,128)(2,1)S(1)} %slice.162), channel_id=1, source_target_pairs={{0,16},{16,0},{1,17},{17,1},{2,18},{18,2},{3,19},{19,3},{4,20},{20... | collective-permute-start | bytes 786440 | tf_op jit(solution)/shard_map/ppermute | solution.py:732
  370.8 23.3 %collective-permute-start.49 = (bf16[144,512]{1,0:T(8,128)(2,1)S(1)}, bf16[144,512]{1,0:T(8,128)(2,1)S(1)}, u32[]{:S(2)}, u32[]{:S(2)}) collective-permute-start(bf16[144,512]{1,0:T(8,128)(2,1)S(1)} %fusion.25), channel_id=1, source_target_pairs={{0,16},{16,0},{1,17},{17,1},{2,18},{18,2},{3,19},{19,3},{4,20},{20... | collective-permute-start | bytes 442376 | tf_op jit(solution)/shard_map/ppermute | solution.py:732
  (94 other events, 1137.6 us)
Sparse Core Ops, SparseCore 0:
  10.2 55.9 all-gather.7
  68.3 58.7 all-gather.9
  128.7 44.6 all-gather.5
  205.9 42.5 reduce-scatter.3
  255.0 42.6 reduce-scatter.5
  321.6 57.7 reduce-scatter.7
